TPU v7x, 256 devices: a whole 4x4x8 slice. The times are simulated.
256 devices in a mesh: dp: 64 (over z_lo, y, x), mp: 4 (over z_hi, core).
Axes of the slice: x: 4, y: 4, z: 8 (z_hi: 2, z_lo: 4; z = z_hi * 4 + z_lo), core: 2. Of those that a mesh axis runs over, the one named last changes fastest.
Arguments:
- tokens: bfloat16 [16384, 8192], P('dp', 'mp'), may hold values from -8 to 8
- attn_gain: bfloat16 [8192], replicated, may hold values from 0.5 to 1.5
- w_query: bfloat16 [8192, 4096], P('dp', 'mp'), may hold values from -2 to 2
- key_projection_weight: bfloat16 [8192, 512], P('dp', 'mp'), may hold values from -2 to 2
- value_projection_weight: bfloat16 [8192, 512], P('dp', 'mp'), may hold values from -0.0625 to 0.0625
- w_out: bfloat16 [4096, 8192], P('mp', 'dp'), may hold values from -0.09375 to 0.09375
- final_gain: bfloat16 [8192], P('mp'), may hold values from 0.5 to 1.5
- unembed: bfloat16 [64128, 8192], P('dp', 'mp'), may hold values from -0.29882812 to 0.29882812
- clean_ids: int32 [64], replicated, may hold values from 0 to 64127, as said below
- corrupt_ids: int32 [64], replicated, may hold values from 0 to 64127
Outputs:
- head_out: bfloat16 [16384, 4096], P('dp', 'mp')
- scores: float32 [64, 32], P('dp', 'mp')
- metric: float32 [64], P('dp')
Inputs may be any that keep to these rules, and one draw needn't show every extreme that they name: `clean_ids`: split the ids into 64 aligned blocks of equal size and number the groups of 1 sequence alike; the block of a clean answer, minus the number of its sequence's group, taken modulo the number of blocks, is drawn so that every such offset occurs for some sequence.
All inputs are finite; a program needn't handle non-finite values.
Results may differ from a plain program's by a relative error of at most 0.015.
Values may be sent and summed in bfloat16 or wider, within the bound.
No kernel may reach another device: no remote copies, remote signals or barrier semaphores. Data moves between devices by JAX's collectives and lax.ppermute only.
A program may use at most 128 MiB of HBM per device.

v0:
```python
import math

import jax
import jax.numpy as jnp
from jax import lax
from jax.sharding import PartitionSpec as P

MODEL_WIDTH = 8192
HEAD_SIZE = 128
SEQUENCE_LENGTH = 256


def side_by_side(arrays, axis, dim, along):
    ends, at = ([], 0)
    for a in arrays[:-1]:
        at += a.shape[along]
        ends.append(at)
    both = jnp.concatenate(arrays, axis=along)
    return tuple(jnp.split(lax.all_gather(both, axis, axis=dim, tiled=True), ends, axis=along))


def from_everyone(value, axis):
    count = lax.axis_size(axis)
    return lax.all_to_all(
        jnp.broadcast_to(value[None], (count, *value.shape)), axis, 0, 0, tiled=True
    )


def of_everyone(value, axis):
    return from_everyone(value, axis).sum(axis=0)


def joined_along(parts, dim):
    parts = jnp.moveaxis(parts, 0, dim)
    lengths = parts.shape
    return parts.reshape(*lengths[:dim], lengths[dim] * lengths[dim + 1], *lengths[dim + 2 :])


def gather_directly(value, axis, dim):
    return joined_along(from_everyone(value, axis), dim)


def of_everyone_2(value, axis):
    everything = from_everyone(value, axis)
    return jnp.sum(everything.astype(jnp.float32), axis=0)


def cut_along(value, dim, count):
    lengths = value.shape
    parts = value.reshape(*lengths[:dim], count, lengths[dim] // count, *lengths[dim + 1 :])
    return jnp.moveaxis(parts, dim, 0)


def summed_on_arrival(value, axis, dim):
    count = lax.axis_size(axis)
    parts = lax.all_to_all(cut_along(value, dim, count), axis, 0, 0, tiled=True)
    return jnp.sum(parts, axis=0)


def together(arrays, axis):
    ends = [0]
    for a in arrays:
        ends.append(ends[-1] + a.size)
    subtotal = of_everyone(jnp.concatenate([a.ravel() for a in arrays]), axis)
    return tuple((subtotal[b:e].reshape(a.shape) for a, b, e in zip(arrays, ends, ends[1:])))


def apply_rotary(tensor, length):
    half_dim = tensor.shape[-1] // 2
    positions = jnp.arange(length, dtype=jnp.float32)
    inv_freq = jnp.exp(
        jnp.arange(half_dim, dtype=jnp.float32) * (-2.0 * math.log(500000.0) / tensor.shape[-1])
    )
    angles = positions[:, None] * inv_freq[None, :]
    cosine_table = jnp.cos(angles)[:, None, :]
    sine_table = jnp.sin(angles)[:, None, :]
    lower_half = tensor[..., :half_dim]
    upper_half = tensor[..., half_dim:]
    return jnp.concatenate(
        [
            lower_half * cosine_table - upper_half * sine_table,
            upper_half * cosine_table + lower_half * sine_table,
        ],
        axis=-1,
    )


def per_device(
    tokens,
    attn_gain,
    w_query,
    key_projection_weight,
    value_projection_weight,
    w_out,
    final_gain,
    unembed,
    clean_ids,
    corrupt_ids,
):
    row_count = tokens.shape[0]
    seq_count = row_count // SEQUENCE_LENGTH
    gathered = lax.all_gather(tokens, "mp", axis=1, tiled=True)
    wide = gathered.astype(jnp.float32)
    normalized_rows = (
        wide
        * lax.rsqrt(jnp.mean(wide * wide, axis=1, keepdims=True) + 1e-05)
        * attn_gain.astype(jnp.float32)
    ).astype(jnp.bfloat16)
    weight_pieces = side_by_side(
        (w_query, key_projection_weight, value_projection_weight), "dp", 0, 1
    )
    query_raw, key_raw, value_raw = tuple(
        (
            jnp.dot(normalized_rows, weight_piece, preferred_element_type=jnp.float32)
            for weight_piece in weight_pieces
        )
    )
    q_heads = query_raw.shape[1] // HEAD_SIZE
    kv_heads = key_raw.shape[1] // HEAD_SIZE
    query_group_width = q_heads // kv_heads
    queries = apply_rotary(
        query_raw.reshape(seq_count, SEQUENCE_LENGTH, q_heads, HEAD_SIZE), SEQUENCE_LENGTH
    ).astype(jnp.bfloat16)
    projected_key_rows = apply_rotary(
        key_raw.reshape(seq_count, SEQUENCE_LENGTH, kv_heads, HEAD_SIZE), SEQUENCE_LENGTH
    ).astype(jnp.bfloat16)
    value_rows = value_raw.astype(jnp.bfloat16).reshape(
        seq_count, SEQUENCE_LENGTH, kv_heads, HEAD_SIZE
    )
    grouped = queries.reshape(seq_count, SEQUENCE_LENGTH, kv_heads, query_group_width, HEAD_SIZE)
    logits = jnp.einsum(
        "btkgd,bskd->bkgts", grouped, projected_key_rows, preferred_element_type=jnp.float32
    ) / math.sqrt(HEAD_SIZE)
    causal = jnp.arange(SEQUENCE_LENGTH)[:, None] >= jnp.arange(SEQUENCE_LENGTH)[None, :]
    logits = jnp.where(causal, logits, -1e30)
    row_top = jnp.max(logits, axis=-1, keepdims=True)
    exponent = jnp.exp(logits - row_top)
    attn_probs = (exponent / jnp.sum(exponent, axis=-1, keepdims=True)).astype(jnp.bfloat16)
    mixed_heads = jnp.einsum(
        "bkgts,bskd->btkgd", attn_probs, value_rows, preferred_element_type=jnp.float32
    )
    head_out = mixed_heads.astype(jnp.bfloat16).reshape(row_count, q_heads * HEAD_SIZE)
    totals = jnp.sum(head_out.astype(jnp.float32), axis=0)
    all_totals = of_everyone(totals, "dp")
    head_mean = all_totals / (row_count * lax.axis_size("dp"))
    last_out = head_out.reshape(seq_count, SEQUENCE_LENGTH, q_heads * HEAD_SIZE)[
        :, SEQUENCE_LENGTH - 1, :
    ]
    every_last = gather_directly(last_out, "dp", 0)
    partial_out = jnp.dot(every_last, w_out, preferred_element_type=jnp.float32)
    summed_out = of_everyone_2(partial_out.astype(jnp.bfloat16), "mp").astype(jnp.float32)
    moved_out = lax.all_to_all(
        summed_out.astype(jnp.bfloat16), "dp", split_axis=0, concat_axis=1, tiled=True
    )
    span = moved_out.shape[1] // lax.axis_size("mp")
    attn_last = lax.dynamic_slice_in_dim(moved_out, lax.axis_index("mp") * span, span, 1)
    last_tokens = tokens.reshape(seq_count, SEQUENCE_LENGTH, tokens.shape[1])[
        :, SEQUENCE_LENGTH - 1, :
    ].astype(jnp.float32)
    residual = last_tokens + attn_last.astype(jnp.float32)
    vocab_rows = unembed.shape[0]
    id_range = lax.axis_index("dp") * vocab_rows + jnp.arange(vocab_rows, dtype=jnp.int32)
    one_hot = (clean_ids[:, None] == id_range[None, :]).astype(jnp.float32) - (
        corrupt_ids[:, None] == id_range[None, :]
    ).astype(jnp.float32)
    direction = summed_on_arrival(
        jnp.dot(one_hot.astype(jnp.bfloat16), unembed, preferred_element_type=jnp.float32), "dp", 0
    )
    weighted = final_gain.astype(jnp.float32) * direction
    square_part, product_part = together(
        (jnp.sum(residual * residual, axis=1), jnp.sum(residual * weighted, axis=1)), "mp"
    )
    inverse = lax.rsqrt(square_part / MODEL_WIDTH + 1e-05)
    metric = inverse * product_part
    grad_last = (
        weighted * inverse[:, None] - residual * (metric * inverse * inverse / MODEL_WIDTH)[:, None]
    ).astype(jnp.bfloat16)
    grad_full = gather_directly(grad_last, "mp", 1)
    grad_seqs = lax.all_to_all(grad_full, "dp", split_axis=1, concat_axis=0, tiled=True)
    head_grads = summed_on_arrival(
        lax.dot_general(
            grad_seqs, w_out, (((1,), (1,)), ((), ())), preferred_element_type=jnp.float32
        ),
        "dp",
        0,
    )
    mean_gap = head_mean[None, :] - last_out.astype(jnp.float32)
    scores = jnp.sum((mean_gap * head_grads).reshape(seq_count, q_heads, HEAD_SIZE), axis=2)
    return (head_out, scores, metric)


def solution(mesh):
    in_specs = (
        P("dp", "mp"),
        P(),
        P("dp", "mp"),
        P("dp", "mp"),
        P("dp", "mp"),
        P("mp", "dp"),
        P("mp"),
        P("dp", "mp"),
        P(),
        P(),
    )
    out_specs = (P("dp", "mp"), P("dp", "mp"), P("dp"))
    return jax.shard_map(
        per_device, mesh=mesh, in_specs=in_specs, out_specs=out_specs, check_vma=False
    )
```

profile of v0, /device:TPU:1, one launch (start us, length us, event | category | flops | bytes accessed | tf_op | source)
XLA Modules:
  0.0 636.5 jit_solution(4554884628780977542)
XLA Ops:
  8.0 1.7 pad_maximum_fusion
  11.0 69.6 %all-gather.3.cloned.1.call-done = bf16[256,8192]{1,0:T(8,128)(2,1)} async-done(((bf16[256,2048]{1,0:T(8,128)(2,1)}), bf16[256,8192]{1,0:T(8,128)(2,1)}) %all-gather.3.cloned.1.call-update) | async-done | bytes 4194320 | tf_op jit(solution)/shard_map/all_gather | solution.py:102
  80.6 3.1 fusion.2
  83.7 344.2 %all-gather.5.cloned.1.call-done = bf16[8192,1280]{1,0:T(8,128)(2,1)} async-done(((bf16[128,1280]{1,0:T(8,128)(2,1)}), bf16[8192,1280]{1,0:T(8,128)(2,1)}) %all-gather.5.cloned.1.call-update) | async-done | bytes 20971536 | tf_op jit(solution)/shard_map/all_gather | solution.py:19
  428.0 9.4 %fusion.10 = f32[32,8,8,128]{3,1,2,0:T(8,128)S(1)} fusion(bf16[8192,1280]{1,0:T(8,128)(2,1)} %all-gather.5.cloned.1.call-done, bf16[256,8192]{1,0:T(8,128)(2,1)} %all-gather.3.cloned.1.call-done, f32[8192]{0:T(1024)S(1)} %convert_element_type.90, f32[256]{0:T(256)S(1)} %add_rsqrt_fusion), kind=kOutput, calls=%fused_computation.16 | convolution fusion | flops 4303355904 | bytes 22053888 | tf_op jit(solution)/shard_map/dot_general | solution.py:114
  437.9 1.6 copy-done.1
  439.5 3.3 fusion.13
  444.6 4.8 convert_reduce_fusion
  450.4 1.4 reduce.15
  452.5 6.8 %all-to-all-start.2 = ((bf16[64,2,512]{2,1,0:T(2,128)(2,1)}), bf16[64,2,512]{2,1,0:T(2,128)(2,1)S(1)}, u32[]{:S(2)}, u32[]{:S(2)}) async-start(bf16[64,2,512]{2,1,0:T(2,128)(2,1)} %reshape.299), calls=%async_computation.2 | async-start | bytes 262144 | tf_op jit(solution)/shard_map/all_to_all | solution.py:24
  459.3 3.1 convolution_bitcast_fusion
  462.4 1.3 copy.63
  463.7 5.1 all-to-all-done.2
  468.8 4.9 all-to-all-start.1
  474.1 12.4 %all-to-all-done.1 = f32[64,1,2048]{2,1,0:T(1,128)S(1)} async-done(((f32[64,1,2048]{2,1,0:T(1,128)}), f32[64,1,2048]{2,1,0:T(1,128)S(1)}, u32[]{:S(2)}, u32[]{:S(2)}) %all-to-all-start.1) | async-done | bytes 524320 | tf_op jit(solution)/shard_map/all_to_all | solution.py:56
  487.1 47.0 %all-to-all-start.3 = ((bf16[4,64,128]{2,1,0:T(8,128)(2,1)}), bf16[4,64,128]{2,1,0:T(8,128)(2,1)S(1)}, u32[]{:S(2)}, u32[]{:S(2)}) async-start(bf16[4,64,128]{2,1,0:T(8,128)(2,1)} %broadcast_in_dim.30), calls=%async_computation.3 | async-start | bytes 131072 | tf_op jit(solution)/shard_map/all_to_all | solution.py:24
  534.4 6.8 %all-to-all-done.3 = bf16[4,64,128]{2,1,0:T(8,128)(2,1)S(1)} async-done(((bf16[4,64,128]{2,1,0:T(8,128)(2,1)}), bf16[4,64,128]{2,1,0:T(8,128)(2,1)S(1)}, u32[]{:S(2)}, u32[]{:S(2)}) %all-to-all-start.3) | async-done | bytes 65568 | tf_op jit(solution)/shard_map/all_to_all | solution.py:24
  541.9 4.7 all-to-all-start.4
  546.5 8.9 %all-to-all-done.4 = bf16[64,1,128]{2,1,0:T(2,128)(2,1)S(1)} async-done(((bf16[64,1,128]{2,1,0:T(2,128)(2,1)}), bf16[64,1,128]{2,1,0:T(2,128)(2,1)S(1)}, u32[]{:S(2)}, u32[]{:S(2)}) %all-to-all-start.4) | async-done | bytes 16416 | tf_op jit(solution)/shard_map/all_to_all | solution.py:152
  555.4 1.4 multiply_reduce_fusion.1
  556.8 1.4 pad_maximum_fusion.1
  558.2 11.6 %all_to_all.69 = f32[4,1,2]{2,1,0:T(1,128)S(1)} all-to-all(f32[4,1,2]{2,1,0:T(1,128)S(1)} %broadcast_in_dim.31), channel_id=1, replica_groups=mesh['dp'=64,'mp'=4] {'mp'}, dimensions={0} | all-to-all | bytes 64 | tf_op jit(solution)/shard_map/all_to_all | solution.py:24
  571.8 0.7 reduce.16
  572.6 10.1 %all_to_all.70 = bf16[4,2,1024]{2,1,0:T(2,128)(2,1)S(1)} all-to-all(bf16[4,2,1024]{2,1,0:T(2,128)(2,1)S(1)} %reshape.301), channel_id=1, replica_groups=mesh['dp'=64,'mp'=4] {'mp'}, dimensions={0} | all-to-all | bytes 32768 | tf_op jit(solution)/shard_map/all_to_all | solution.py:24
  582.7 12.8 %all_to_all.71 = bf16[1,64,128]{2,0,1:T(2,128)(2,1)S(1)} all-to-all(bf16[1,64,128]{2,0,1:T(2,128)(2,1)S(1)} %bitcast.88), channel_id=1, replica_groups=mesh['dp'=64,'mp'=4] {'dp'}, dimensions={1} | all-to-all | bytes 32768 | tf_op jit(solution)/shard_map/all_to_all | solution.py:179
  595.5 0.8 broadcast_in_dim.27
  596.3 4.6 all-to-all-start
  601.2 1.0 copy.67
  602.1 9.5 %all-to-all-done = f32[64,1,1024]{2,1,0:T(1,128)S(1)} async-done(((f32[64,1,1024]{2,1,0:T(1,128)}), f32[64,1,1024]{2,1,0:T(1,128)S(1)}, u32[]{:S(2)}, u32[]{:S(2)}) %all-to-all-start) | async-done | bytes 262176 | tf_op jit(solution)/shard_map/all_to_all | solution.py:24
  611.6 5.3 all-to-all-start.8
  617.1 1.0 copy.68
  618.3 9.3 %all-to-all-done.8 = f32[64,1,1024]{2,1,0:T(1,128)S(1)} async-done(((f32[64,1,1024]{2,1,0:T(1,128)}), f32[64,1,1024]{2,1,0:T(1,128)S(1)}, u32[]{:S(2)}, u32[]{:S(2)}) %all-to-all-start.8) | async-done | bytes 262176 | tf_op jit(solution)/shard_map/all_to_all | solution.py:56
  (49 shorter events, 9.9 us)
Async XLA Ops:
  7.2 466.7 %copy-start = (bf16[1024,128]{1,0:T(8,128)(2,1)S(1)}, bf16[1024,128]{1,0:T(8,128)(2,1)}, u32[]{:S(2)}) copy-start(bf16[1024,128]{1,0:T(8,128)(2,1)} %param.15) | copy-start | bytes 786436
  7.2 73.4 %all-gather.3.cloned.1.call-start = ((), (), s32[]{:S(2)}) async-start(), calls=%async_computation.9 | async-start | bytes 5242880 | tf_op jit(solution)/shard_map/all_gather | solution.py:102
  7.9 420.1 %all-gather.5.cloned.1.call-start = ((), (), s32[]{:S(2)}) async-start(), calls=%async_computation.10 | async-start | bytes 21299200 | tf_op jit(solution)/shard_map/all_gather | solution.py:19
  437.3 2.2 copy-start.1
  444.6 14.7 %copy-start.3 = (s32[64]{0:T(128)S(1)}, s32[64]{0:T(128)}, u32[]{:S(2)}) copy-start(s32[64]{0:T(128)} %param.19) | copy-start | bytes 772
  444.6 14.7 %copy-start.4 = (s32[64]{0:T(128)S(1)}, s32[64]{0:T(128)}, u32[]{:S(2)}) copy-start(s32[64]{0:T(128)} %param.18) | copy-start | bytes 772
  452.5 16.3 %all-to-all-start.2 = ((bf16[64,2,512]{2,1,0:T(2,128)(2,1)}), bf16[64,2,512]{2,1,0:T(2,128)(2,1)S(1)}, u32[]{:S(2)}, u32[]{:S(2)}) async-start(bf16[64,2,512]{2,1,0:T(2,128)(2,1)} %reshape.299), calls=%async_computation.2 | async-start | bytes 262144 | tf_op jit(solution)/shard_map/all_to_all | solution.py:24
  459.3 87.2 %copy-start.2 = (bf16[2048]{0:T(1024)(128)(2,1)S(1)}, bf16[2048]{0:T(1024)(128)(2,1)}, u32[]{:S(2)}) copy-start(bf16[2048]{0:T(1024)(128)(2,1)} %param.16) | copy-start | bytes 12292
  468.8 17.6 %all-to-all-start.1 = ((f32[64,1,2048]{2,1,0:T(1,128)}), f32[64,1,2048]{2,1,0:T(1,128)S(1)}, u32[]{:S(2)}, u32[]{:S(2)}) async-start(f32[64,1,2048]{2,1,0:T(1,128)} %copy.63), calls=%async_computation.1 | async-start | bytes 1048576 | tf_op jit(solution)/shard_map/all_to_all | solution.py:56
  487.1 54.1 %all-to-all-start.3 = ((bf16[4,64,128]{2,1,0:T(8,128)(2,1)}), bf16[4,64,128]{2,1,0:T(8,128)(2,1)S(1)}, u32[]{:S(2)}, u32[]{:S(2)}) async-start(bf16[4,64,128]{2,1,0:T(8,128)(2,1)} %broadcast_in_dim.30), calls=%async_computation.3 | async-start | bytes 131072 | tf_op jit(solution)/shard_map/all_to_all | solution.py:24
  541.9 13.6 %all-to-all-start.4 = ((bf16[64,1,128]{2,1,0:T(2,128)(2,1)}), bf16[64,1,128]{2,1,0:T(2,128)(2,1)S(1)}, u32[]{:S(2)}, u32[]{:S(2)}) async-start(bf16[64,1,128]{2,1,0:T(2,128)(2,1)} %copy.64), calls=%async_computation.4 | async-start | bytes 65536 | tf_op jit(solution)/shard_map/all_to_all | solution.py:152
  596.3 15.3 %all-to-all-start = ((f32[64,1,1024]{2,1,0:T(1,128)}), f32[64,1,1024]{2,1,0:T(1,128)S(1)}, u32[]{:S(2)}, u32[]{:S(2)}) async-start(f32[64,1,1024]{2,1,0:T(1,128)} %broadcast_in_dim.27), calls=%async_computation | async-start | bytes 524288 | tf_op jit(solution)/shard_map/all_to_all | solution.py:24
  611.6 16.1 %all-to-all-start.8 = ((f32[64,1,1024]{2,1,0:T(1,128)}), f32[64,1,1024]{2,1,0:T(1,128)S(1)}, u32[]{:S(2)}, u32[]{:S(2)}) async-start(f32[64,1,1024]{2,1,0:T(1,128)} %copy.67), calls=%async_computation.8 | async-start | bytes 524288 | tf_op jit(solution)/shard_map/all_to_all | solution.py:56
Sparse Core Ops, SparseCore 0:
  9.8 70.7 all-gather.2
  83.0 344.9 all-gather.4
where the time goes:
time: 639 us; the launch traced here: 636 us
  waiting for transfers between devices  467 us (73%)
  starting transfers between devices  73.4 us (11%)
  blocking collectives  34.4 us (5%)
  matrix products  21.6 us (3%)
  between operations  16.8 us (3%)
  other arithmetic  13.7 us (2%)
  local copies, waits for them, and re-layouts  9.94 us (2%)
    all_gather x1, waiting for transfers between devices, side_by_side(): lax.all_gather(both, axis, axis=dim, tiled=True)  344 us
    all_gather x1, waiting for transfers between devices, per_device(): gathered = lax.all_gather(tokens, 'mp', axis=1, tiled=True)  69.6 us
    all_to_all x3, starting transfers between devices, from_everyone(): lax.all_to_all(jnp.broadcast_to(value[None], (count, *value.shape)), axis...  58.4 us
    all_to_all x2, waiting for transfers between devices, summed_on_arrival(): parts = lax.all_to_all(cut_along(value, dim, count), axis, 0, 0, tiled=True)  21.7 us
    all_to_all x2, blocking collectives, from_everyone(): lax.all_to_all(jnp.broadcast_to(value[None], (count, *value.shape)), axis...  21.7 us
    all_to_all x3, waiting for transfers between devices, from_everyone(): lax.all_to_all(jnp.broadcast_to(value[None], (count, *value.shape)), axis...  21.4 us
    all_to_all x1, blocking collectives, per_device(): lax.all_to_all(grad_full, 'dp', split_axis=1, concat_axis=0, tiled=True)  12.8 us
  transfers between devices with their start and end apart: 8, of which 8 were waited for; matrix products, arithmetic and copies ran while one was open for 2% of the time, Pallas kernels for 0%

commit v1 on v0

v1 whole, which is shorter than its diff:
```python
import math

import jax
import jax.numpy as jnp
from jax import lax
from jax.sharding import Mesh, PartitionSpec as P

MODEL_WIDTH = 8192
HEAD_SIZE = 128
LENGTH = 256
TOKENS = 16384
DP = ("zl", "y", "x")
MP = ("zh", "c")
F32 = jnp.float32
BF16 = jnp.bfloat16


def from_everyone(value, axis):
    count = lax.axis_size(axis)
    return lax.all_to_all(
        jnp.broadcast_to(value[None], (count, *value.shape)), axis, 0, 0, tiled=True
    )


def send(value, route):
    pairs = []
    for x in range(4):
        for c in range(2):
            to = route(x, c)
            if to is not None:
                pairs.append((x * 2 + c, (to[0] % 4) * 2 + to[1]))
    return lax.ppermute(value, ("x", "c"), pairs)


def rotary_tables():
    half = HEAD_SIZE // 2
    positions = jnp.arange(LENGTH, dtype=F32)
    inv_freq = jnp.exp(
        jnp.arange(half, dtype=F32) * (-2.0 * math.log(500000.0) / HEAD_SIZE)
    )
    angles = positions[:, None] * inv_freq[None, :]
    return jnp.cos(angles)[:, None, :], jnp.sin(angles)[:, None, :]


def rotate(t, cos, sin):
    half = HEAD_SIZE // 2
    lo, hi = t[..., :half], t[..., half:]
    return jnp.concatenate([lo * cos - hi * sin, hi * cos + lo * sin], axis=-1)


def ring_share(block, core):
    pa = send(block, lambda x, c: (x - 1, 0) if c == 0 else (x + 1, 1))
    pb = send(block, lambda x, c: (x + 1, 1) if c == 0 else (x - 1, 0))
    pc = send(block, lambda x, c: (x + 2, 1) if c == 0 else (x, 0))
    pd = send(block, lambda x, c: None if c == 0 else (x + 2, 1))
    first = core == 0
    f0 = jnp.concatenate([jnp.where(first, block, pc), jnp.where(first, pa, pb)], axis=0)
    f1 = jnp.concatenate([jnp.where(first, pc, pd), jnp.where(first, pb, pa)], axis=0)
    return f0, f1


def per_device(tokens, gain, w_query, w_key, w_value, w_out, final_gain, unembed, clean, corrupt):
    zh, core, x = lax.axis_index("zh"), lax.axis_index("c"), lax.axis_index("x")
    odd = x % 2

    with jax.named_scope("weights"):
        wkv = jnp.concatenate([w_key, w_value], axis=1)
        width = w_query.shape[1] // 2
        mine = lax.dynamic_slice_in_dim(w_query, odd * width, width, 1)
        other = lax.dynamic_slice_in_dim(w_query, (1 - odd) * width, width, 1)
        pa = send(jnp.concatenate([mine, wkv], axis=1), lambda x, c: (2 * c + x % 2, x // 2))
        pb = send(jnp.concatenate([other, wkv], axis=1), lambda x, c: (2 * c + 1 - x % 2, x // 2))
        rows = jnp.concatenate(
            [jnp.where(odd == 0, pa, pb), jnp.where(odd == 0, pb, pa)], axis=0
        )
        along_z = lax.all_gather(rows, "zl", axis=0)
        order = [2 * zh, 2 * zh + 1, 2 - 2 * zh, 3 - 2 * zh]
        weights = [
            lax.all_gather(
                lax.dynamic_index_in_dim(along_z, m, 0, keepdims=False),
                ("y", "c"),
                axis=0,
                tiled=True,
            )
            for m in order
        ]

    with jax.named_scope("tokens"):
        far = lax.ppermute(tokens, "zh", [(0, 1), (1, 0)])
        chunks = ring_share(tokens, core) + ring_share(far, core)

    with jax.named_scope("direction"):
        vocab_rows = unembed.shape[0]
        dp_index = lax.axis_index(DP)
        ids = dp_index * vocab_rows + jnp.arange(vocab_rows, dtype=jnp.int32)
        one_hot = (clean[:, None] == ids[None, :]).astype(F32) - (
            corrupt[:, None] == ids[None, :]
        ).astype(F32)
        found = jnp.dot(one_hot.astype(BF16), unembed, preferred_element_type=F32)
        direction = jnp.sum(lax.all_to_all(found[:, None], DP, 0, 0, tiled=True), axis=0)
        weighted = final_gain.astype(F32) * direction[0]
        both = jnp.stack([weighted, tokens[LENGTH - 1].astype(F32)])
        wide = jnp.moveaxis(from_everyone(both, MP), 0, 1).reshape(2, 64, 128)
        columns = lax.all_to_all(jnp.moveaxis(wide, 1, 0), DP, 0, 0, tiled=True)
        weighted_cols, token_cols = columns[:, 0], columns[:, 1]
        back_w = lax.dot_general(
            weighted_cols.astype(BF16), w_out, (((1,), (1,)), ((), ())), preferred_element_type=F32
        )
        grad_w = jnp.sum(lax.all_to_all(back_w[:, None], DP, 0, 0, tiled=True), axis=0)[0]

    with jax.named_scope("project"):
        acc, squares = 0.0, 0.0
        for m, chunk, weight in zip(order, chunks, weights):
            t = chunk.astype(F32)
            g = lax.dynamic_slice_in_dim(gain, m * t.shape[1], t.shape[1], 0).astype(F32)
            squares = squares + jnp.sum(t * t, axis=1, keepdims=True)
            acc = acc + jnp.dot((t * g).astype(BF16), weight, preferred_element_type=F32)
        acc = acc * lax.rsqrt(squares / MODEL_WIDTH + 1e-05)
        heads = width // HEAD_SIZE
        acc = acc.reshape(2, LENGTH, heads + 2, HEAD_SIZE)
        cos, sin = rotary_tables()
        queries = rotate(acc[:, :, :heads], cos, sin).astype(BF16)
        keys = rotate(acc[:, :, heads : heads + 1], cos, sin)[:, :, 0].astype(BF16)
        values = acc[:, :, heads + 1].astype(BF16)

    with jax.named_scope("attend"):
        logits = jnp.einsum("btgd,bsd->bgts", queries, keys, preferred_element_type=F32)
        logits = logits / math.sqrt(HEAD_SIZE)
        causal = jnp.arange(LENGTH)[:, None] >= jnp.arange(LENGTH)[None, :]
        logits = jnp.where(causal, logits, -1e30)
        top = jnp.max(logits, axis=-1, keepdims=True)
        e = jnp.exp(logits - top)
        probs = (e / jnp.sum(e, axis=-1, keepdims=True)).astype(BF16)
        mixed = jnp.einsum("bgts,bsd->btgd", probs, values, preferred_element_type=F32)
        mixed = mixed.astype(BF16).reshape(2, LENGTH, width)

    with jax.named_scope("return_heads"):
        oa = send(mixed[0], lambda x, c: (x, x // 2) if c == 0 else (x + 2, x // 2))
        ob = send(mixed[1], lambda x, c: (x + 1, x // 2) if c == 0 else (x - 1, x // 2))
        head_out = jnp.concatenate(
            [jnp.where(odd == 0, oa, ob), jnp.where(odd == 0, ob, oa)], axis=1
        )

    with jax.named_scope("tail"):
        last = head_out[LENGTH - 1].astype(F32)
        total = jnp.sum(head_out.astype(F32), axis=0)
        every = from_everyone(jnp.stack([last, total]), DP)
        head_mean = jnp.sum(every[:, 1], axis=0) / TOKENS
        part = jnp.dot(every[:, 0].astype(BF16), w_out, preferred_element_type=F32)
        attn_last = jnp.sum(from_everyone(part, MP), axis=0).astype(BF16)
        residual = token_cols + attn_last.astype(F32)
        back_r = lax.dot_general(
            residual.astype(BF16), w_out, (((1,), (1,)), ((), ())), preferred_element_type=F32
        )
        sums = jnp.concatenate(
            [
                jnp.broadcast_to(jnp.sum(residual * residual, axis=1)[:, None], (64, 64)),
                jnp.broadcast_to(jnp.sum(residual * weighted_cols, axis=1)[:, None], (64, 64)),
            ],
            axis=1,
        )
        packed = jnp.concatenate([back_r, sums], axis=1)
        mine = jnp.sum(lax.all_to_all(packed[:, None], DP, 0, 0, tiled=True), axis=0)[0]
        grad_r, square, product = mine[:1024], mine[1024], mine[1024 + 64]
        inverse = lax.rsqrt(square / MODEL_WIDTH + 1e-05)
        metric = inverse * product
        head_grads = grad_w * inverse - grad_r * (metric * inverse * inverse / MODEL_WIDTH)
        scores = jnp.sum(((head_mean - last) * head_grads).reshape(1, 8, HEAD_SIZE), axis=2)
    return head_out, scores, metric[None]


def solution(mesh):
    fine = Mesh(mesh.devices.reshape(4, 4, 4, 2, 2), (*DP, *MP))
    in_specs = (
        P(DP, MP),
        P(),
        P(DP, MP),
        P(DP, MP),
        P(DP, MP),
        P(MP, DP),
        P(MP),
        P(DP, MP),
        P(),
        P(),
    )
    out_specs = (P(DP, MP), P(DP, MP), P(DP))
    return jax.shard_map(
        per_device, mesh=fine, in_specs=in_specs, out_specs=out_specs, check_vma=False
    )
```

time: 639 us -> 344 us (0.54)
  waiting for transfers between devices: 467 us -> 189 us
  blocking collectives: 34.4 us -> 0 us
  matrix products: 21.6 us -> 31.5 us
  local copies, waits for them, and re-layouts: 9.94 us -> 18.8 us
    all_gather x2 -> x5, waiting for transfers between devices: 414 us -> 43.2 us  [the longest x1 43.2 us: per_device(): along_z = lax.all_gather(rows, 'zl', axis=0)]
    ppermute x0 -> x13, waiting for transfers between devices: none -> 51.8 us  [the longest x12 51.8 us: send(): return lax.ppermute(value, ('x', 'c'), pairs)]
    all_to_all x3, starting transfers between devices: 58.4 us -> 16.9 us  [from_everyone(): lax.all_to_all(jnp.broadcast_to(value[None], (count, *value.shape)), axis...]
    all_to_all x3 -> x4, waiting for transfers between devices: 30.6 us -> 68.6 us  [the longest x1 39.4 us: per_device(): lax.all_to_all(found[:, None], DP, 0, 0, tiled=True)]
    all_to_all x3 -> x0, blocking collectives: 34.4 us -> none  [the longest x2 21.7 us: from_everyone(): lax.all_to_all(jnp.broadcast_to(value[None], (count, *value.shape)), axis...]
    ppermute x0 -> x13, starting transfers between devices: none -> 28.2 us  [the longest x12 24.1 us: send(): return lax.ppermute(value, ('x', 'c'), pairs)]
    all_to_all x3 -> x4, starting transfers between devices: 14.9 us -> 24.9 us  [the longest x1 7.85 us: per_device(): lax.all_to_all(found[:, None], DP, 0, 0, tiled=True)]
    dot_general x7 -> x9, matrix products: 21.6 us -> 28.1 us  [the longest x4 22.3 us: per_device(): jnp.dot((t * g).astype(BF16), weight, preferred_element_type=F32)]
  transfers between devices with their start and end apart: 8 -> 25, of which waited for: 8 -> 15; matrix products, arithmetic and copies ran while one was open for 2% -> 10% of each run, Pallas kernels for 0% -> 0%
where the time goes in v1:
time: 344 us; the launch traced here: 342 us
  waiting for transfers between devices  189 us (55%)
  starting transfers between devices  70.2 us (20%)
  matrix products  31.5 us (9%)
  local copies, waits for them, and re-layouts  18.8 us (5%)
  between operations  16.8 us (5%)
  other arithmetic  15.5 us (5%)
    ppermute x12, waiting for transfers between devices, send(): return lax.ppermute(value, ('x', 'c'), pairs)  51.8 us
    all_gather x1, waiting for transfers between devices, per_device(): along_z = lax.all_gather(rows, 'zl', axis=0)  43.2 us
    all_to_all x1, waiting for transfers between devices, per_device(): lax.all_to_all(found[:, None], DP, 0, 0, tiled=True)  39.4 us
    all_to_all x3, waiting for transfers between devices, from_everyone(): lax.all_to_all(jnp.broadcast_to(value[None], (count, *value.shape)), axis...  24.1 us
    ppermute x12, starting transfers between devices, send(): return lax.ppermute(value, ('x', 'c'), pairs)  24.1 us
    dot_general x4, matrix products, per_device(): jnp.dot((t * g).astype(BF16), weight, preferred_element_type=F32)  22.3 us
    all_to_all x3, starting transfers between devices, from_everyone(): lax.all_to_all(jnp.broadcast_to(value[None], (count, *value.shape)), axis...  16.9 us
    all_to_all x1, waiting for transfers between devices, per_device(): lax.all_to_all(packed[:, None], DP, 0, 0, tiled=True)  10.7 us
  transfers between devices with their start and end apart: 25, of which 15 were waited for; matrix products, arithmetic and copies ran while one was open for 10% of the time, Pallas kernels for 0%

profile of v1, /device:TPU:1, one launch (start us, length us, event | category | flops | bytes accessed | tf_op | source)
XLA Modules:
  0.0 341.8 jit_solution(12943895693049163494)
XLA Ops:
  9.1 6.0 %collective-permute-start.3 = (bf16[128,768]{1,0:T(8,128)(2,1)S(1)}, bf16[128,768]{1,0:T(8,128)(2,1)S(1)}, u32[]{:S(2)}, u32[]{:S(2)}) collective-permute-start(bf16[128,768]{1,0:T(8,128)(2,1)S(1)} %get-tuple-element.37), channel_id=1, source_target_pairs={{0,0},{1,8},{4,4},{5,12},{8,1},{9,9},{12,5},{13,13},{2,2},{3,10},{... | collective-permute-start | bytes 589832 | tf_op jit(solution)/shard_map/weights/ppermute | solution.py:32
  15.8 3.7 %collective-permute-done.3 = bf16[128,768]{1,0:T(8,128)(2,1)S(1)} collective-permute-done((bf16[128,768]{1,0:T(8,128)(2,1)S(1)}, bf16[128,768]{1,0:T(8,128)(2,1)S(1)}, u32[]{:S(2)}, u32[]{:S(2)}) %collective-permute-start.3) | collective-permute-done | bytes 196640 | tf_op jit(solution)/shard_map/weights/ppermute | solution.py:32
  19.5 2.1 collective-permute-done.4
  22.5 43.2 %all-gather.11.cloned.1.call-done = bf16[1024,768]{1,0:T(8,128)(2,1)} async-done(((bf16[256,768]{1,0:T(8,128)(2,1)}), bf16[1024,768]{1,0:T(8,128)(2,1)}) %all-gather.11.cloned.1.call-update) | async-done | bytes 1572880 | tf_op jit(solution)/shard_map/weights/all_gather | solution.py:76
  65.7 2.5 constant_dynamic-slice_fusion
  69.6 4.1 %collective-permute-start.6 = (bf16[256,2048]{1,0:T(8,128)(2,1)S(1)}, bf16[256,2048]{1,0:T(8,128)(2,1)}, u32[]{:S(2)}, u32[]{:S(2)}) collective-permute-start(bf16[256,2048]{1,0:T(8,128)(2,1)S(1)} %copy-done.8), channel_id=1, source_target_pairs={{0,2},{2,0},{1,3},{3,1},{4,6},{6,4},{5,7},{7,5},{8,10},{10,8},{9,1... | collective-permute-start | bytes 3145736 | tf_op jit(solution)/shard_map/tokens/ppermute | solution.py:89
  74.5 4.6 %collective-permute-start.5 = (bf16[256,2048]{1,0:T(8,128)(2,1)S(1)}, bf16[256,2048]{1,0:T(8,128)(2,1)}, u32[]{:S(2)}, u32[]{:S(2)}) collective-permute-start(bf16[256,2048]{1,0:T(8,128)(2,1)S(1)} %copy-done.8), channel_id=1, source_target_pairs={{1,9},{5,13},{9,1},{13,5},{3,11},{7,15},{11,3},{15,7},{17,25},{21,... | collective-permute-start | bytes 3145736 | tf_op jit(solution)/shard_map/tokens/ppermute | solution.py:32
  79.1 3.2 convolution_bitcast_fusion
  83.7 7.9 %all-to-all-start.1 = ((f32[64,1,2048]{2,1,0:T(1,128)}), f32[64,1,2048]{2,1,0:T(1,128)S(1)}, u32[]{:S(2)}, u32[]{:S(2)}) async-start(f32[64,1,2048]{2,1,0:T(1,128)} %copy.55), calls=%async_computation.1 | async-start | bytes 1048576 | tf_op jit(solution)/shard_map/direction/all_to_all | solution.py:100
  96.8 39.4 %all-to-all-done.1 = f32[64,1,2048]{2,1,0:T(1,128)S(1)} async-done(((f32[64,1,2048]{2,1,0:T(1,128)}), f32[64,1,2048]{2,1,0:T(1,128)S(1)}, u32[]{:S(2)}, u32[]{:S(2)}) %all-to-all-start.1) | async-done | bytes 524320 | tf_op jit(solution)/shard_map/direction/all_to_all | solution.py:100
  136.5 3.3 collective-permute-start.10
  145.6 38.6 %collective-permute-done.8 = bf16[256,2048]{1,0:T(8,128)(2,1)S(1)} collective-permute-done((bf16[256,2048]{1,0:T(8,128)(2,1)}, bf16[256,2048]{1,0:T(8,128)(2,1)S(1)}, u32[]{:S(2)}, u32[]{:S(2)}) %collective-permute-start.8) | collective-permute-done | bytes 1048608 | tf_op jit(solution)/shard_map/tokens/ppermute | solution.py:32
  184.6 3.0 collective-permute-done.7
  189.7 5.6 %fusion.11 = f32[512,768]{1,0:T(8,128)} fusion(bf16[1,2048,768]{2,1,0:T(8,128)(2,1)} %all-gather.17.cloned.1.call-done, f32[2048]{0:T(1024)} %get-tuple-element.42, bf16[256,2048]{1,0:T(8,128)(2,1)} %copy-done.1, bf16[256,2048]{1,0:T(8,128)(2,1)} %copy-done.6), kind=kOutput, calls=%fused_computation.19 | convolution fusion | flops 1616904192 | bytes 6823936 | tf_op jit(solution)/shard_map/project/dot_general | solution.py:117
  195.3 5.2 %fusion.13 = f32[512,768]{1,0:T(8,128)} fusion(bf16[1,2048,768]{2,1,0:T(8,128)(2,1)} %all-gather.15.cloned.1.call-done, f32[2048]{0:T(1024)} %get-tuple-element.40, bf16[256,2048]{1,0:T(8,128)(2,1)S(1)} %get-tuple-element.11, bf16[256,2048]{1,0:T(8,128)(2,1)} %copy-done.3), kind=kOutput, calls=%fused_computation.21 | convolution fusion | flops 1616904192 | bytes 6823936 | tf_op jit(solution)/shard_map/project/dot_general | solution.py:117
  200.5 5.3 %fusion.15 = f32[512,768]{1,0:T(8,128)} fusion(bf16[1,2048,768]{2,1,0:T(8,128)(2,1)} %all-gather.13.cloned.1.call-done, f32[2048]{0:T(1024)} %get-tuple-element.41, bf16[256,2048]{1,0:T(8,128)(2,1)S(1)} %get-tuple-element.12, bf16[256,2048]{1,0:T(8,128)(2,1)} %copy-done.2), kind=kOutput, calls=%fused_computation.23 | convolution fusion | flops 1616904192 | bytes 6823936 | tf_op jit(solution)/shard_map/project/dot_general | solution.py:117
  205.8 6.3 %add_multiply_fusion = f32[512,768]{1,0:T(8,128)} fusion(f32[512,768]{1,0:T(8,128)} %fusion.11, f32[512,768]{1,0:T(8,128)} %fusion.15, f32[512,768]{1,0:T(8,128)} %fusion.13, bf16[1,2048,768]{2,1,0:T(8,128)(2,1)} %all-gather.19.cloned.1.call-done, f32[2048]{0:T(1024)} %get-tuple-element.39, bf16[256,2048]{1,0:T(8,128)(2,1)S(1)} %get-tuple-element.9, ...), kind=kOutput, calls=%fused_computation.38 | convolution fusion | flops 1618477056 | bytes 11544576 | tf_op jit(solution)/shard_map/project/dot_general | solution.py:117
  222.1 3.5 %fusion.75 = (f32[2,4,256]{2,1,0:T(4,128)S(1)}, f32[2,4,256,256]{2,3,1,0:T(8,128)}) fusion(pred[256,256]{0,1:T(8,128)(4,1)} %iota_compare_fusion, bf16[2,256,4,64]{3,1,2,0:T(8,128)(2,1)} %get-tuple-element.8, bf16[2,256,4,64]{3,1,2,0:T(8,128)(2,1)S(1)} %get-tuple-element.7, bf16[2,256,1,64]{3,1,0,2:T(8,128)(2,1)S(1)} %copy-done.10, ...), kind=kOutput, calls=%fused_computation.132 | convolution fusion | flops 137625856 | bytes 2826240 | tf_op jit(solution)/shard_map/attend/sub | solution.py:132
  227.7 4.0 %collective-permute-start.11 = (bf16[256,512]{1,0:T(8,128)(2,1)S(1)}, bf16[256,512]{1,0:T(8,128)(2,1)S(1)}, u32[]{:S(2)}, u32[]{:S(2)}) collective-permute-start(bf16[256,512]{1,0:T(8,128)(2,1)S(1)} %copy.53), channel_id=1, source_target_pairs={{0,0},{1,8},{4,4},{5,12},{8,9},{9,1},{12,13},{13,5},{2,2},{3,10},{... | collective-permute-start | bytes 786440 | tf_op jit(solution)/shard_map/return_heads/ppermute | solution.py:32
  232.8 3.4 all-to-all-start.2
  236.2 2.7 collective-permute-done.11
  241.4 2.0 all-to-all-done.2
  244.3 7.5 %all-to-all-start = ((f32[64,2,1024]{2,1,0:T(2,128)}), f32[64,2,1024]{2,1,0:T(2,128)S(1)}, u32[]{:S(2)}, u32[]{:S(2)}) async-start(f32[64,2,1024]{2,1,0:T(2,128)} %broadcast_in_dim.26), calls=%async_computation | async-start | bytes 1048576 | tf_op jit(solution)/shard_map/tail/all_to_all | solution.py:20
  252.6 15.8 %all-to-all-done = f32[64,2,1024]{2,1,0:T(2,128)S(1)} async-done(((f32[64,2,1024]{2,1,0:T(2,128)}), f32[64,2,1024]{2,1,0:T(2,128)S(1)}, u32[]{:S(2)}, u32[]{:S(2)}) %all-to-all-start) | async-done | bytes 524320 | tf_op jit(solution)/shard_map/tail/all_to_all | solution.py:20
  268.3 5.7 %all-to-all-start.3 = ((f32[64,2,128]{2,1,0:T(2,128)}), f32[64,2,128]{2,1,0:T(2,128)S(1)}, u32[]{:S(2)}, u32[]{:S(2)}) async-start(f32[64,2,128]{2,1,0:T(2,128)} %copy.57), calls=%async_computation.3 | async-start | bytes 131072 | tf_op jit(solution)/shard_map/direction/all_to_all | solution.py:104
  274.4 8.8 %all-to-all-done.3 = f32[64,2,128]{2,1,0:T(2,128)S(1)} async-done(((f32[64,2,128]{2,1,0:T(2,128)}), f32[64,2,128]{2,1,0:T(2,128)S(1)}, u32[]{:S(2)}, u32[]{:S(2)}) %all-to-all-start.3) | async-done | bytes 65568 | tf_op jit(solution)/shard_map/direction/all_to_all | solution.py:104
  283.8 6.1 %all-to-all-start.5 = ((f32[4,64,128]{2,1,0:T(8,128)}), f32[4,64,128]{2,1,0:T(8,128)S(1)}, u32[]{:S(2)}, u32[]{:S(2)}) async-start(f32[4,64,128]{2,1,0:T(8,128)} %broadcast_in_dim.30), calls=%async_computation.5 | async-start | bytes 262144 | tf_op jit(solution)/shard_map/tail/all_to_all | solution.py:20
  291.2 6.3 %all-to-all-done.5 = f32[4,64,128]{2,1,0:T(8,128)S(1)} async-done(((f32[4,64,128]{2,1,0:T(8,128)}), f32[4,64,128]{2,1,0:T(8,128)S(1)}, u32[]{:S(2)}, u32[]{:S(2)}) %all-to-all-start.5) | async-done | bytes 131104 | tf_op jit(solution)/shard_map/tail/all_to_all | solution.py:20
  297.4 5.6 %all-to-all-start.4 = ((f32[64,1,1024]{2,1,0:T(1,128)}), f32[64,1,1024]{2,1,0:T(1,128)S(1)}, u32[]{:S(2)}, u32[]{:S(2)}) async-start(f32[64,1,1024]{2,1,0:T(1,128)} %copy.59), calls=%async_computation.4 | async-start | bytes 524288 | tf_op jit(solution)/shard_map/direction/all_to_all | solution.py:109
  304.6 9.7 %all-to-all-done.4 = f32[64,1,1024]{2,1,0:T(1,128)S(1)} async-done(((f32[64,1,1024]{2,1,0:T(1,128)}), f32[64,1,1024]{2,1,0:T(1,128)S(1)}, u32[]{:S(2)}, u32[]{:S(2)}) %all-to-all-start.4) | async-done | bytes 262176 | tf_op jit(solution)/shard_map/direction/all_to_all | solution.py:109
  314.3 5.8 %all-to-all-start.6 = ((f32[64,1,1152]{2,1,0:T(1,128)}), f32[64,1,1152]{2,1,0:T(1,128)S(1)}, u32[]{:S(2)}, u32[]{:S(2)}) async-start(f32[64,1,1152]{2,1,0:T(1,128)} %copy.62), calls=%async_computation.6 | async-start | bytes 589824 | tf_op jit(solution)/shard_map/tail/all_to_all | solution.py:163
  320.7 10.7 %all-to-all-done.6 = f32[64,1,1152]{2,1,0:T(1,128)S(1)} async-done(((f32[64,1,1152]{2,1,0:T(1,128)}), f32[64,1,1152]{2,1,0:T(1,128)S(1)}, u32[]{:S(2)}, u32[]{:S(2)}) %all-to-all-start.6) | async-done | bytes 294944 | tf_op jit(solution)/shard_map/tail/all_to_all | solution.py:163
  (125 shorter events, 43.5 us)
Async XLA Ops:
  7.2 267.0 %copy-start = (bf16[1024,128]{1,0:T(8,128)(2,1)S(1)}, bf16[1024,128]{1,0:T(8,128)(2,1)}, u32[]{:S(2)}) copy-start(bf16[1024,128]{1,0:T(8,128)(2,1)} %param.15) | copy-start | bytes 786436
  7.2 58.5 %all-gather.11.cloned.1.call-start = ((), (), s32[]{:S(2)}) async-start(), calls=%async_computation.7 | async-start | bytes 1966080 | tf_op jit(solution)/shard_map/weights/all_gather | solution.py:76
  9.1 10.4 %collective-permute-start.3 = (bf16[128,768]{1,0:T(8,128)(2,1)S(1)}, bf16[128,768]{1,0:T(8,128)(2,1)S(1)}, u32[]{:S(2)}, u32[]{:S(2)}) collective-permute-start(bf16[128,768]{1,0:T(8,128)(2,1)S(1)} %get-tuple-element.37), channel_id=1, source_target_pairs={{0,0},{1,8},{4,4},{5,12},{8,1},{9,9},{12,5},{13,13},{2,2},{3,10},{... | collective-permute-start | bytes 589832 | tf_op jit(solution)/shard_map/weights/ppermute | solution.py:32
  15.1 6.5 %collective-permute-start.4 = (bf16[128,768]{1,0:T(8,128)(2,1)S(1)}, bf16[128,768]{1,0:T(8,128)(2,1)S(1)}, u32[]{:S(2)}, u32[]{:S(2)}) collective-permute-start(bf16[128,768]{1,0:T(8,128)(2,1)S(1)} %get-tuple-element.38), channel_id=1, source_target_pairs={{0,4},{1,12},{4,0},{5,8},{8,5},{9,13},{12,1},{13,9},{2,6},{3,14},{... | collective-permute-start | bytes 589832 | tf_op jit(solution)/shard_map/weights/ppermute | solution.py:32
  15.8 53.8 %copy-start.8 = (bf16[256,2048]{1,0:T(8,128)(2,1)S(1)}, bf16[256,2048]{1,0:T(8,128)(2,1)}, u32[]{:S(2)}) copy-start(bf16[256,2048]{1,0:T(8,128)(2,1)} %param.10) | copy-start | bytes 3145732
  21.6 57.5 %copy-start.13 = (s32[64]{0:T(128)S(1)}, s32[64]{0:T(128)}, u32[]{:S(2)}) copy-start(s32[64]{0:T(128)} %param.19) | copy-start | bytes 772
  21.6 57.5 %copy-start.14 = (s32[64]{0:T(128)S(1)}, s32[64]{0:T(128)}, u32[]{:S(2)}) copy-start(s32[64]{0:T(128)} %param.18) | copy-start | bytes 772
  22.4 167.3 %all-gather.17.cloned.1.call-start = ((), (), s32[]{:S(2)}) async-start(), calls=%async_computation.10 | async-start | bytes 3538944 | tf_op jit(solution)/shard_map/weights/all_gather | solution.py:79
  68.2 127.1 %all-gather.15.cloned.1.call-start = ((), (), s32[]{:S(2)}) async-start(), calls=%async_computation.9 | async-start | bytes 3538944 | tf_op jit(solution)/shard_map/weights/all_gather | solution.py:79
  69.0 131.5 %all-gather.13.cloned.1.call-start = ((), (), s32[]{:S(2)}) async-start(), calls=%async_computation.8 | async-start | bytes 3538944 | tf_op jit(solution)/shard_map/weights/all_gather | solution.py:79
  69.6 136.3 %all-gather.19.cloned.1.call-start = ((), (), s32[]{:S(2)}) async-start(), calls=%async_computation.11 | async-start | bytes 3538944 | tf_op jit(solution)/shard_map/weights/all_gather | solution.py:79
  69.6 66.9 %collective-permute-start.6 = (bf16[256,2048]{1,0:T(8,128)(2,1)S(1)}, bf16[256,2048]{1,0:T(8,128)(2,1)}, u32[]{:S(2)}, u32[]{:S(2)}) collective-permute-start(bf16[256,2048]{1,0:T(8,128)(2,1)S(1)} %copy-done.8), channel_id=1, source_target_pairs={{0,2},{2,0},{1,3},{3,1},{4,6},{6,4},{5,7},{7,5},{8,10},{10,8},{9,1... | collective-permute-start | bytes 3145736 | tf_op jit(solution)/shard_map/tokens/ppermute | solution.py:89
  73.7 66.1 %collective-permute-start = (bf16[256,2048]{1,0:T(8,128)(2,1)S(1)}, bf16[256,2048]{1,0:T(8,128)(2,1)}, u32[]{:S(2)}, u32[]{:S(2)}) collective-permute-start(bf16[256,2048]{1,0:T(8,128)(2,1)S(1)} %copy-done.8), channel_id=1, source_target_pairs={{0,9},{1,0},{4,13},{5,4},{8,1},{9,8},{12,5},{13,12},{2,11},{3,2},{... | collective-permute-start | bytes 3145736 | tf_op jit(solution)/shard_map/tokens/ppermute | solution.py:32
  74.5 65.5 %collective-permute-start.5 = (bf16[256,2048]{1,0:T(8,128)(2,1)S(1)}, bf16[256,2048]{1,0:T(8,128)(2,1)}, u32[]{:S(2)}, u32[]{:S(2)}) collective-permute-start(bf16[256,2048]{1,0:T(8,128)(2,1)S(1)} %copy-done.8), channel_id=1, source_target_pairs={{1,9},{5,13},{9,1},{13,5},{3,11},{7,15},{11,3},{15,7},{17,25},{21,... | collective-permute-start | bytes 3145736 | tf_op jit(solution)/shard_map/tokens/ppermute | solution.py:32
  79.1 17.0 %copy-start.11 = (bf16[8192]{0:T(1024)(128)(2,1)S(1)}, bf16[8192]{0:T(1024)(128)(2,1)}, u32[]{:S(2)}) copy-start(bf16[8192]{0:T(1024)(128)(2,1)} %param.11) | copy-start | bytes 49156
  83.7 52.5 %all-to-all-start.1 = ((f32[64,1,2048]{2,1,0:T(1,128)}), f32[64,1,2048]{2,1,0:T(1,128)S(1)}, u32[]{:S(2)}, u32[]{:S(2)}) async-start(f32[64,1,2048]{2,1,0:T(1,128)} %copy.55), calls=%async_computation.1 | async-start | bytes 1048576 | tf_op jit(solution)/shard_map/direction/all_to_all | solution.py:100
  91.6 50.2 %collective-permute-start.1 = (bf16[256,2048]{1,0:T(8,128)(2,1)S(1)}, bf16[256,2048]{1,0:T(8,128)(2,1)S(1)}, u32[]{:S(2)}, u32[]{:S(2)}) collective-permute-start(bf16[256,2048]{1,0:T(8,128)(2,1)S(1)} %copy-done.8), channel_id=1, source_target_pairs={{0,12},{1,5},{4,0},{5,9},{8,4},{9,13},{12,8},{13,1},{2,14},{3,7},{... | collective-permute-start | bytes 3145736 | tf_op jit(solution)/shard_map/tokens/ppermute | solution.py:32
  92.7 50.6 %collective-permute-start.2 = (bf16[256,2048]{1,0:T(8,128)(2,1)S(1)}, bf16[256,2048]{1,0:T(8,128)(2,1)}, u32[]{:S(2)}, u32[]{:S(2)}) collective-permute-start(bf16[256,2048]{1,0:T(8,128)(2,1)S(1)} %copy-done.8), channel_id=1, source_target_pairs={{0,5},{1,12},{4,9},{5,0},{8,13},{9,4},{12,1},{13,8},{2,7},{3,14},{... | collective-permute-start | bytes 3145736 | tf_op jit(solution)/shard_map/tokens/ppermute | solution.py:32
  136.5 48.0 %collective-permute-start.10 = (bf16[256,2048]{1,0:T(8,128)(2,1)}, bf16[256,2048]{1,0:T(8,128)(2,1)S(1)}, u32[]{:S(2)}, u32[]{:S(2)}) collective-permute-start(bf16[256,2048]{1,0:T(8,128)(2,1)} %collective-permute-done.6), channel_id=1, source_target_pairs={{1,9},{5,13},{9,1},{13,5},{3,11},{7,15},{11,3},{15,7},{17,25},{21,... | collective-permute-start | bytes 3145736 | tf_op jit(solution)/shard_map/tokens/ppermute | solution.py:32
  139.9 44.4 %collective-permute-start.8 = (bf16[256,2048]{1,0:T(8,128)(2,1)}, bf16[256,2048]{1,0:T(8,128)(2,1)S(1)}, u32[]{:S(2)}, u32[]{:S(2)}) collective-permute-start(bf16[256,2048]{1,0:T(8,128)(2,1)} %collective-permute-done.6), channel_id=1, source_target_pairs={{0,12},{1,5},{4,0},{5,9},{8,4},{9,13},{12,8},{13,1},{2,14},{3,7},{... | collective-permute-start | bytes 3145736 | tf_op jit(solution)/shard_map/tokens/ppermute | solution.py:32
  140.0 44.4 %collective-permute-start.9 = (bf16[256,2048]{1,0:T(8,128)(2,1)}, bf16[256,2048]{1,0:T(8,128)(2,1)S(1)}, u32[]{:S(2)}, u32[]{:S(2)}) collective-permute-start(bf16[256,2048]{1,0:T(8,128)(2,1)} %collective-permute-done.6), channel_id=1, source_target_pairs={{0,5},{1,12},{4,9},{5,0},{8,13},{9,4},{12,1},{13,8},{2,7},{3,14},{... | collective-permute-start | bytes 3145736 | tf_op jit(solution)/shard_map/tokens/ppermute | solution.py:32
  141.8 45.7 %collective-permute-start.7 = (bf16[256,2048]{1,0:T(8,128)(2,1)}, bf16[256,2048]{1,0:T(8,128)(2,1)S(1)}, u32[]{:S(2)}, u32[]{:S(2)}) collective-permute-start(bf16[256,2048]{1,0:T(8,128)(2,1)} %collective-permute-done.6), channel_id=1, source_target_pairs={{0,9},{1,0},{4,13},{5,4},{8,1},{9,8},{12,5},{13,12},{2,11},{3,2},{... | collective-permute-start | bytes 3145736 | tf_op jit(solution)/shard_map/tokens/ppermute | solution.py:32
  200.5 5.3 %copy-start.5 = (bf16[256,2048]{1,0:T(8,128)(2,1)S(1)}, bf16[256,2048]{1,0:T(8,128)(2,1)}, u32[]{:S(2)}) copy-start(bf16[256,2048]{1,0:T(8,128)(2,1)} %copy-done.4) | copy-start | bytes 3145732
  225.5 6.6 %copy-start.12 = (bf16[2048]{0:T(1024)(128)(2,1)S(1)}, bf16[2048]{0:T(1024)(128)(2,1)}, u32[]{:S(2)}) copy-start(bf16[2048]{0:T(1024)(128)(2,1)} %param.16) | copy-start | bytes 12292
  227.7 11.2 %collective-permute-start.11 = (bf16[256,512]{1,0:T(8,128)(2,1)S(1)}, bf16[256,512]{1,0:T(8,128)(2,1)S(1)}, u32[]{:S(2)}, u32[]{:S(2)}) collective-permute-start(bf16[256,512]{1,0:T(8,128)(2,1)S(1)} %copy.53), channel_id=1, source_target_pairs={{0,0},{1,8},{4,4},{5,12},{8,9},{9,1},{12,13},{13,5},{2,2},{3,10},{... | collective-permute-start | bytes 786440 | tf_op jit(solution)/shard_map/return_heads/ppermute | solution.py:32
  231.8 8.6 %collective-permute-start.12 = (bf16[256,512]{1,0:T(8,128)(2,1)S(1)}, bf16[256,512]{1,0:T(8,128)(2,1)S(1)}, u32[]{:S(2)}, u32[]{:S(2)}) collective-permute-start(bf16[256,512]{1,0:T(8,128)(2,1)S(1)} %copy.54), channel_id=1, source_target_pairs={{0,4},{1,12},{4,8},{5,0},{8,13},{9,5},{12,1},{13,9},{2,6},{3,14},{... | collective-permute-start | bytes 786440 | tf_op jit(solution)/shard_map/return_heads/ppermute | solution.py:32
  232.8 10.6 %all-to-all-start.2 = ((f32[4,2,2048]{2,1,0:T(2,128)}), f32[4,2,2048]{2,1,0:T(2,128)S(1)}, u32[]{:S(2)}, u32[]{:S(2)}) async-start(f32[4,2,2048]{2,1,0:T(2,128)} %broadcast_in_dim.28), calls=%async_computation.2 | async-start | bytes 131072 | tf_op jit(solution)/shard_map/direction/all_to_all | solution.py:20
  244.3 24.0 %all-to-all-start = ((f32[64,2,1024]{2,1,0:T(2,128)}), f32[64,2,1024]{2,1,0:T(2,128)S(1)}, u32[]{:S(2)}, u32[]{:S(2)}) async-start(f32[64,2,1024]{2,1,0:T(2,128)} %broadcast_in_dim.26), calls=%async_computation | async-start | bytes 1048576 | tf_op jit(solution)/shard_map/tail/all_to_all | solution.py:20
  268.3 14.8 %all-to-all-start.3 = ((f32[64,2,128]{2,1,0:T(2,128)}), f32[64,2,128]{2,1,0:T(2,128)S(1)}, u32[]{:S(2)}, u32[]{:S(2)}) async-start(f32[64,2,128]{2,1,0:T(2,128)} %copy.57), calls=%async_computation.3 | async-start | bytes 131072 | tf_op jit(solution)/shard_map/direction/all_to_all | solution.py:104
  283.8 13.6 %all-to-all-start.5 = ((f32[4,64,128]{2,1,0:T(8,128)}), f32[4,64,128]{2,1,0:T(8,128)S(1)}, u32[]{:S(2)}, u32[]{:S(2)}) async-start(f32[4,64,128]{2,1,0:T(8,128)} %broadcast_in_dim.30), calls=%async_computation.5 | async-start | bytes 262144 | tf_op jit(solution)/shard_map/tail/all_to_all | solution.py:20
  297.4 16.9 %all-to-all-start.4 = ((f32[64,1,1024]{2,1,0:T(1,128)}), f32[64,1,1024]{2,1,0:T(1,128)S(1)}, u32[]{:S(2)}, u32[]{:S(2)}) async-start(f32[64,1,1024]{2,1,0:T(1,128)} %copy.59), calls=%async_computation.4 | async-start | bytes 524288 | tf_op jit(solution)/shard_map/direction/all_to_all | solution.py:109
  314.3 17.0 %all-to-all-start.6 = ((f32[64,1,1152]{2,1,0:T(1,128)}), f32[64,1,1152]{2,1,0:T(1,128)S(1)}, u32[]{:S(2)}, u32[]{:S(2)}) async-start(f32[64,1,1152]{2,1,0:T(1,128)} %copy.62), calls=%async_computation.6 | async-start | bytes 589824 | tf_op jit(solution)/shard_map/tail/all_to_all | solution.py:163
  (8 other events, 22.5 us)
Sparse Core Ops, SparseCore 0:
  22.6 43.0 all-gather.10
  68.4 30.7 all-gather.16
  101.0 34.3 all-gather.14
  137.1 30.4 all-gather.12
  169.3 30.3 all-gather.18

commit v2 on v1

--- a/solution.py
+++ b/solution.py
@@ -49,11 +49,11 @@
 
 
 def ring_share(block, core):
+    first = core == 0
     pa = send(block, lambda x, c: (x - 1, 0) if c == 0 else (x + 1, 1))
     pb = send(block, lambda x, c: (x + 1, 1) if c == 0 else (x - 1, 0))
-    pc = send(block, lambda x, c: (x + 2, 1) if c == 0 else (x, 0))
-    pd = send(block, lambda x, c: None if c == 0 else (x + 2, 1))
-    first = core == 0
+    pc = send(jnp.where(first, pa, block), lambda x, c: (x - 1, 1) if c == 0 else (x, 0))
+    pd = send(pa, lambda x, c: None if c == 0 else (x + 1, 1))
     f0 = jnp.concatenate([jnp.where(first, block, pc), jnp.where(first, pa, pb)], axis=0)
     f1 = jnp.concatenate([jnp.where(first, pc, pd), jnp.where(first, pb, pa)], axis=0)
     return f0, f1
@@ -73,17 +73,7 @@
         rows = jnp.concatenate(
             [jnp.where(odd == 0, pa, pb), jnp.where(odd == 0, pb, pa)], axis=0
         )
-        along_z = lax.all_gather(rows, "zl", axis=0)
-        order = [2 * zh, 2 * zh + 1, 2 - 2 * zh, 3 - 2 * zh]
-        weights = [
-            lax.all_gather(
-                lax.dynamic_index_in_dim(along_z, m, 0, keepdims=False),
-                ("y", "c"),
-                axis=0,
-                tiled=True,
-            )
-            for m in order
-        ]
+        weights = lax.all_gather(rows, ("zl", "y", "c"), axis=0, tiled=True)
 
     with jax.named_scope("tokens"):
         far = lax.ppermute(tokens, "zh", [(0, 1), (1, 0)])
@@ -108,13 +98,23 @@
         )
         grad_w = jnp.sum(lax.all_to_all(back_w[:, None], DP, 0, 0, tiled=True), axis=0)[0]
 
-    with jax.named_scope("project"):
-        acc, squares = 0.0, 0.0
-        for m, chunk, weight in zip(order, chunks, weights):
+    with jax.named_scope("scale"):
+        order = [2 * zh, 2 * zh + 1, 2 - 2 * zh, 3 - 2 * zh]
+        scaled, squares = [], 0.0
+        for m, chunk in zip(order, chunks):
             t = chunk.astype(F32)
             g = lax.dynamic_slice_in_dim(gain, m * t.shape[1], t.shape[1], 0).astype(F32)
             squares = squares + jnp.sum(t * t, axis=1, keepdims=True)
-            acc = acc + jnp.dot((t * g).astype(BF16), weight, preferred_element_type=F32)
+            scaled.append((t * g).astype(BF16))
+        *scaled, squares, weights, weighted_cols, token_cols, grad_w = lax.optimization_barrier(
+            (*scaled, squares, weights, weighted_cols, token_cols, grad_w)
+        )
+
+    with jax.named_scope("project"):
+        acc, depth = 0.0, scaled[0].shape[1]
+        for m, t in zip(order, scaled):
+            weight = lax.dynamic_slice_in_dim(weights, m * depth, depth, 0)
+            acc = acc + jnp.dot(t, weight, preferred_element_type=F32)
         acc = acc * lax.rsqrt(squares / MODEL_WIDTH + 1e-05)
         heads = width // HEAD_SIZE
         acc = acc.reshape(2, LENGTH, heads + 2, HEAD_SIZE)

time: 344 us -> 301 us (0.88)
  waiting for transfers between devices: 189 us -> 116 us
  blocking collectives: 0 us -> 38.4 us
  other arithmetic: 15.5 us -> 26.4 us
  matrix products: 31.5 us -> 21 us
  starting transfers between devices: 70.2 us -> 64.9 us
  local copies, waits for them, and re-layouts: 18.8 us -> 15.3 us
    all_gather x5 -> x1, waiting for transfers between devices: 43.2 us -> 0.01 us  [per_device(): weights = lax.all_gather(rows, ('zl', 'y', 'c'), axis=0, tiled=True)]
    all_to_all x0 -> x2, blocking collectives: none -> 38.4 us  [from_everyone(): lax.all_to_all(jnp.broadcast_to(value[None], (count, *value.shape)), axis...]
    ppermute x12, waiting for transfers between devices: 51.8 us -> 17.1 us  [send(): return lax.ppermute(value, ('x', 'c'), pairs)]
    all_to_all x3 -> x1, waiting for transfers between devices: 24.1 us -> 0.01 us  [from_everyone(): lax.all_to_all(jnp.broadcast_to(value[None], (count, *value.shape)), axis...]
    ppermute x1, waiting for transfers between devices: 0.01 us -> 19.7 us  [per_device(): far = lax.ppermute(tokens, 'zh', [(0, 1), (1, 0)])]
    all_to_all x1, waiting for transfers between devices: 39.4 us -> 51.8 us  [per_device(): lax.all_to_all(found[:, None], DP, 0, 0, tiled=True)]
    dot_general x4, matrix products: 22.3 us -> 12 us  [per_device(): acc = acc + jnp.dot(t, weight, preferred_element_type=F32)]
    all_to_all x3 -> x1, starting transfers between devices: 16.9 us -> 7.7 us  [from_everyone(): lax.all_to_all(jnp.broadcast_to(value[None], (count, *value.shape)), axis...]
  transfers between devices with their start and end apart: 25 -> 19, of which waited for: 15 -> 11; matrix products, arithmetic and copies ran while one was open for 10% -> 10% of each run, Pallas kernels for 0% -> 0%
where the time goes in v2:
time: 301 us; the launch traced here: 299 us
  waiting for transfers between devices  116 us (39%)
  starting transfers between devices  64.9 us (22%)
  blocking collectives  38.4 us (13%)
  other arithmetic  26.4 us (9%)
  matrix products  21 us (7%)
  between operations  17.1 us (6%)
  local copies, waits for them, and re-layouts  15.3 us (5%)
    all_to_all x1, waiting for transfers between devices, per_device(): lax.all_to_all(found[:, None], DP, 0, 0, tiled=True)  51.8 us
    all_to_all x2, blocking collectives, from_everyone(): lax.all_to_all(jnp.broadcast_to(value[None], (count, *value.shape)), axis...  38.4 us
    ppermute x12, starting transfers between devices, send(): return lax.ppermute(value, ('x', 'c'), pairs)  24.7 us
    ppermute x1, waiting for transfers between devices, per_device(): far = lax.ppermute(tokens, 'zh', [(0, 1), (1, 0)])  19.7 us
    ppermute x12, waiting for transfers between devices, send(): return lax.ppermute(value, ('x', 'c'), pairs)  17.1 us
    all_to_all x1, waiting for transfers between devices, per_device(): columns = lax.all_to_all(jnp.moveaxis(wide, 1, 0), DP, 0, 0, tiled=True)  12.6 us
    dot_general x4, matrix products, per_device(): acc = acc + jnp.dot(t, weight, preferred_element_type=F32)  12 us
    all_to_all x1, waiting for transfers between devices, per_device(): lax.all_to_all(packed[:, None], DP, 0, 0, tiled=True)  11.2 us
  transfers between devices with their start and end apart: 19, of which 11 were waited for; matrix products, arithmetic and copies ran while one was open for 10% of the time, Pallas kernels for 0%

profile of v2, /device:TPU:1, one launch (start us, length us, event | category | flops | bytes accessed | tf_op | source)
XLA Modules:
  0.0 299.4 jit_solution(7528856795557269202)
XLA Ops:
  9.1 4.0 %collective-permute-start.10 = (bf16[128,768]{1,0:T(8,128)(2,1)S(1)}, bf16[128,768]{1,0:T(8,128)(2,1)S(1)}, u32[]{:S(2)}, u32[]{:S(2)}) collective-permute-start(bf16[128,768]{1,0:T(8,128)(2,1)S(1)} %get-tuple-element.62), channel_id=1, source_target_pairs={{0,4},{1,12},{4,0},{5,8},{8,5},{9,13},{12,1},{13,9},{2,6},{3,14},{... | collective-permute-start | bytes 589832 | tf_op jit(solution)/shard_map/weights/ppermute | solution.py:32
  13.0 2.2 collective-permute-start.9
  16.4 5.1 %collective-permute-done.9 = bf16[128,768]{1,0:T(8,128)(2,1)S(1)} collective-permute-done((bf16[128,768]{1,0:T(8,128)(2,1)S(1)}, bf16[128,768]{1,0:T(8,128)(2,1)S(1)}, u32[]{:S(2)}, u32[]{:S(2)}) %collective-permute-start.9) | collective-permute-done | bytes 196640 | tf_op jit(solution)/shard_map/weights/ppermute | solution.py:32
  22.4 3.1 %convolution_bitcast_fusion = f32[64,1,2048]{2,0,1:T(8,128)S(1)} fusion(bf16[1002,2048]{1,0:T(8,128)(2,1)} %param.17, s32[1002]{0:T(1024)S(1)} %iota_add_fusion, s32[64]{0:T(128)S(1)} %copy-done.21, s32[64]{0:T(128)S(1)} %copy-done.22), kind=kOutput, calls=%fused_computation.25 | convolution fusion | flops 263053056 | bytes 4633000 | tf_op jit(solution)/shard_map/direction/dot_general | solution.py:89
  26.8 9.3 %all-to-all-start = ((f32[64,1,2048]{2,1,0:T(1,128)}), f32[64,1,2048]{2,1,0:T(1,128)S(1)}, u32[]{:S(2)}, u32[]{:S(2)}) async-start(f32[64,1,2048]{2,1,0:T(1,128)} %copy.46), calls=%async_computation | async-start | bytes 1048576 | tf_op jit(solution)/shard_map/direction/all_to_all | solution.py:90
  36.1 4.3 %collective-permute-start.4 = (bf16[256,2048]{1,0:T(8,128)(2,1)S(1)}, bf16[256,2048]{1,0:T(8,128)(2,1)S(1)}, u32[]{:S(2)}, u32[]{:S(2)}) collective-permute-start(bf16[256,2048]{1,0:T(8,128)(2,1)S(1)} %copy-done.1), channel_id=1, source_target_pairs={{0,2},{2,0},{1,3},{3,1},{4,6},{6,4},{5,7},{7,5},{8,10},{10,8},{9,1... | collective-permute-start | bytes 3145736 | tf_op jit(solution)/shard_map/tokens/ppermute | solution.py:79
  41.4 2.9 collective-permute-start.2
  45.5 51.8 %all-to-all-done = f32[64,1,2048]{2,1,0:T(1,128)S(1)} async-done(((f32[64,1,2048]{2,1,0:T(1,128)}), f32[64,1,2048]{2,1,0:T(1,128)S(1)}, u32[]{:S(2)}, u32[]{:S(2)}) %all-to-all-start) | async-done | bytes 524320 | tf_op jit(solution)/shard_map/direction/all_to_all | solution.py:90
  98.3 7.7 %all-to-all-start.1 = ((f32[4,2,2048]{2,1,0:T(2,128)}), f32[4,2,2048]{2,1,0:T(2,128)S(1)}, u32[]{:S(2)}, u32[]{:S(2)}) async-start(f32[4,2,2048]{2,1,0:T(2,128)} %broadcast_in_dim.25), calls=%async_computation.1 | async-start | bytes 131072 | tf_op jit(solution)/shard_map/direction/all_to_all | solution.py:20
  106.0 19.7 %collective-permute-done.4 = bf16[256,2048]{1,0:T(8,128)(2,1)S(1)} collective-permute-done((bf16[256,2048]{1,0:T(8,128)(2,1)S(1)}, bf16[256,2048]{1,0:T(8,128)(2,1)S(1)}, u32[]{:S(2)}, u32[]{:S(2)}) %collective-permute-start.4) | collective-permute-done | bytes 1048608 | tf_op jit(solution)/shard_map/tokens/ppermute | solution.py:79
  126.7 3.5 %collective-permute-start.7 = (bf16[256,2048]{1,0:T(8,128)(2,1)S(1)}, bf16[256,2048]{1,0:T(8,128)(2,1)}, u32[]{:S(2)}, u32[]{:S(2)}) collective-permute-start(bf16[256,2048]{1,0:T(8,128)(2,1)S(1)} %collective-permute-done.4), channel_id=1, source_target_pairs={{0,5},{1,12},{4,9},{5,0},{8,13},{9,4},{12,1},{13,8},{2,7},{3,14},{... | collective-permute-start | bytes 3145736 | tf_op jit(solution)/shard_map/tokens/ppermute | solution.py:32
  131.7 5.5 %all-to-all-start.2 = ((f32[64,2,128]{2,1,0:T(2,128)}), f32[64,2,128]{2,1,0:T(2,128)}, u32[]{:S(2)}, u32[]{:S(2)}) async-start(f32[64,2,128]{2,1,0:T(2,128)} %copy.48), calls=%async_computation.2 | async-start | bytes 131072 | tf_op jit(solution)/shard_map/direction/all_to_all | solution.py:94
  137.2 3.2 %broadcast_select_fusion.5 = (bf16[256,2048]{1,0:T(8,128)(2,1)S(1)}, bf16[256,2048]{1,0:T(8,128)(2,1)}, bf16[256,2048]{1,0:T(8,128)(2,1)}) fusion(bf16[256,2048]{1,0:T(8,128)(2,1)} %collective-permute-done.2, bf16[256,2048]{1,0:T(8,128)(2,1)} %collective-permute-done, pred[]{:T(512)S(6)} %eq.17, bf16[256,2048]{1,0:T(8,128)(2,1)S(1)} %copy-done.1), kind=kLoop, calls=%fused_computation.49 | loop fusion | flops 1572864 | bytes 6291457 | tf_op jit(solution)/shard_map/tokens/jit(_where)/select_n | solution.py:58
  140.3 2.7 collective-permute-start.3
  143.0 12.6 %all-to-all-done.2 = f32[64,2,128]{2,1,0:T(2,128)} async-done(((f32[64,2,128]{2,1,0:T(2,128)}), f32[64,2,128]{2,1,0:T(2,128)}, u32[]{:S(2)}, u32[]{:S(2)}) %all-to-all-start.2) | async-done | bytes 65568 | tf_op jit(solution)/shard_map/direction/all_to_all | solution.py:94
  159.0 7.8 %all-to-all-start.3 = ((f32[64,1,1024]{2,1,0:T(1,128)}), f32[64,1,1024]{2,1,0:T(1,128)}, u32[]{:S(2)}, u32[]{:S(2)}) async-start(f32[64,1,1024]{2,1,0:T(1,128)} %copy.51), calls=%async_computation.3 | async-start | bytes 524288 | tf_op jit(solution)/shard_map/direction/all_to_all | solution.py:99
  166.8 3.3 %broadcast_select_fusion = (bf16[256,2048]{1,0:T(8,128)(2,1)}, bf16[256,2048]{1,0:T(8,128)(2,1)}, bf16[256,2048]{1,0:T(8,128)(2,1)}) fusion(bf16[256,2048]{1,0:T(8,128)(2,1)} %collective-permute-done.7, bf16[256,2048]{1,0:T(8,128)(2,1)} %collective-permute-done.5, pred[]{:T(512)S(6)} %eq.17, bf16[256,2048]{1,0:T(8,128)(2,1)S(1)} %collective-permute-done.4), kind=kLoop, calls=%fused_computation.44 | loop fusion | flops 1572864 | bytes 6291457 | tf_op jit(solution)/shard_map/tokens/jit(_where)/select_n | solution.py:58
  170.6 3.3 %collective-permute-start.8 = (bf16[256,2048]{1,0:T(8,128)(2,1)}, bf16[256,2048]{1,0:T(8,128)(2,1)}, u32[]{:S(2)}, u32[]{:S(2)}) collective-permute-start(bf16[256,2048]{1,0:T(8,128)(2,1)} %collective-permute-done.5), channel_id=1, source_target_pairs={{1,5},{5,9},{9,13},{13,1},{3,7},{7,11},{11,15},{15,3},{17,21},{21,... | collective-permute-start | bytes 3145736 | tf_op jit(solution)/shard_map/tokens/ppermute | solution.py:32
  174.5 4.0 %all-to-all-done.3 = f32[64,1,1024]{2,1,0:T(1,128)} async-done(((f32[64,1,1024]{2,1,0:T(1,128)}), f32[64,1,1024]{2,1,0:T(1,128)}, u32[]{:S(2)}, u32[]{:S(2)}) %all-to-all-start.3) | async-done | bytes 262176 | tf_op jit(solution)/shard_map/direction/all_to_all | solution.py:99
  182.1 2.6 fusion.2
  185.3 2.5 collective-permute-done.8
  189.6 2.7 fusion.6
  192.3 3.8 %fusion.13 = f32[512,768]{1,0:T(8,128)S(1)} fusion(bf16[512,2048]{1,0:T(8,128)(2,1)S(1)} %copy-done.6, bf16[8192,768]{1,0:T(8,128)(2,1)} %all-gather.2.cloned.1.call-done, s32[]{:T(128)S(6)} %select_n.110), kind=kOutput, calls=%fused_computation.21 | convolution fusion | flops 1610612736 | bytes 6815748 | tf_op jit(solution)/shard_map/project/dot_general | solution.py:117
  196.1 4.5 %fusion.11 = f32[512,768]{1,0:T(8,128)S(1)} fusion(bf16[512,2048]{1,0:T(8,128)(2,1)S(1)} %copy-done.8, bf16[8192,768]{1,0:T(8,128)(2,1)} %all-gather.2.cloned.1.call-done, s32[]{:T(128)S(6)} %select_n.114), kind=kOutput, calls=%fused_computation.19 | convolution fusion | flops 1610612736 | bytes 6815748 | tf_op jit(solution)/shard_map/project/dot_general | solution.py:117
  213.0 3.4 %fusion.63 = (f32[2,4,256]{2,1,0:T(4,128)S(1)}, f32[2,4,256,256]{2,3,1,0:T(8,128)}) fusion(pred[256,256]{0,1:T(8,128)(4,1)S(1)} %copy-done.15, bf16[2,256,4,64]{3,1,2,0:T(8,128)(2,1)} %get-tuple-element.26, bf16[2,256,4,64]{3,1,2,0:T(8,128)(2,1)S(1)} %get-tuple-element.25, bf16[2,256,1,64]{3,1,0,2:T(8,128)(2,1)S(1)} %copy-done.14, ...), kind=kOutput, calls=%fused_computation.124 | convolution fusion | flops 137625856 | bytes 2826240 | tf_op jit(solution)/shard_map/attend/sub | solution.py:132
  216.4 1.9 fusion.20
  218.5 2.1 collective-permute-start.11
  222.3 6.1 %collective-permute-done.11 = bf16[256,512]{1,0:T(8,128)(2,1)S(1)} collective-permute-done((bf16[256,512]{1,0:T(8,128)(2,1)S(1)}, bf16[256,512]{1,0:T(8,128)(2,1)S(1)}, u32[]{:S(2)}, u32[]{:S(2)}) %collective-permute-start.11) | collective-permute-done | bytes 262176 | tf_op jit(solution)/shard_map/return_heads/ppermute | solution.py:32
  231.1 25.1 %all_to_all.35 = f32[64,2,1024]{2,1,0:T(2,128)S(1)} all-to-all(f32[64,2,1024]{2,1,0:T(2,128)S(1)} %broadcast_in_dim.29), channel_id=1, replica_groups=mesh['zl'=4,'y'=4,'x'=4,'zh'=2,'c'=2] {'zl','y','x'}, dimensions={0} | all-to-all | bytes 1048576 | tf_op jit(solution)/shard_map/tail/all_to_all | solution.py:20
  256.6 13.3 %all_to_all.36 = f32[4,64,128]{2,1,0:T(8,128)S(1)} all-to-all(f32[4,64,128]{2,1,0:T(8,128)S(1)} %broadcast_in_dim.30), channel_id=1, replica_groups=mesh['zl'=4,'y'=4,'x'=4,'zh'=2,'c'=2] {'zh','c'}, dimensions={0} | all-to-all | bytes 262144 | tf_op jit(solution)/shard_map/tail/all_to_all | solution.py:20
  271.5 5.6 %all-to-all-start.6 = ((f32[64,1,1152]{2,1,0:T(1,128)}), f32[64,1,1152]{2,1,0:T(1,128)S(1)}, u32[]{:S(2)}, u32[]{:S(2)}) async-start(f32[64,1,1152]{2,1,0:T(1,128)} %copy.62), calls=%async_computation.6 | async-start | bytes 589824 | tf_op jit(solution)/shard_map/tail/all_to_all | solution.py:163
  277.4 11.2 %all-to-all-done.6 = f32[64,1,1152]{2,1,0:T(1,128)S(1)} async-done(((f32[64,1,1152]{2,1,0:T(1,128)}), f32[64,1,1152]{2,1,0:T(1,128)S(1)}, u32[]{:S(2)}, u32[]{:S(2)}) %all-to-all-start.6) | async-done | bytes 294944 | tf_op jit(solution)/shard_map/tail/all_to_all | solution.py:163
  (129 shorter events, 41.6 us)
Async XLA Ops:
  7.2 150.6 %copy-start = (bf16[1024,128]{1,0:T(8,128)(2,1)S(1)}, bf16[1024,128]{1,0:T(8,128)(2,1)}, u32[]{:S(2)}) copy-start(bf16[1024,128]{1,0:T(8,128)(2,1)} %param.15) | copy-start | bytes 786436
  7.2 15.2 %copy-start.22 = (s32[64]{0:T(128)S(1)}, s32[64]{0:T(128)}, u32[]{:S(2)}) copy-start(s32[64]{0:T(128)} %param.18) | copy-start | bytes 772
  7.2 15.2 %copy-start.21 = (s32[64]{0:T(128)S(1)}, s32[64]{0:T(128)}, u32[]{:S(2)}) copy-start(s32[64]{0:T(128)} %param.19) | copy-start | bytes 772
  7.2 185.0 %all-gather.2.cloned.1.call-start = ((), (), s32[]{:S(2)}) async-start(), calls=%async_computation.7 | async-start | bytes 12976128 | tf_op jit(solution)/shard_map/weights/all_gather | solution.py:76
  9.1 7.3 %collective-permute-start.10 = (bf16[128,768]{1,0:T(8,128)(2,1)S(1)}, bf16[128,768]{1,0:T(8,128)(2,1)S(1)}, u32[]{:S(2)}, u32[]{:S(2)}) collective-permute-start(bf16[128,768]{1,0:T(8,128)(2,1)S(1)} %get-tuple-element.62), channel_id=1, source_target_pairs={{0,4},{1,12},{4,0},{5,8},{8,5},{9,13},{12,1},{13,9},{2,6},{3,14},{... | collective-permute-start | bytes 589832 | tf_op jit(solution)/shard_map/weights/ppermute | solution.py:32
  13.0 8.5 %collective-permute-start.9 = (bf16[128,768]{1,0:T(8,128)(2,1)S(1)}, bf16[128,768]{1,0:T(8,128)(2,1)S(1)}, u32[]{:S(2)}, u32[]{:S(2)}) collective-permute-start(bf16[128,768]{1,0:T(8,128)(2,1)S(1)} %get-tuple-element.61), channel_id=1, source_target_pairs={{0,0},{1,8},{4,4},{5,12},{8,1},{9,9},{12,5},{13,13},{2,2},{3,10},{... | collective-permute-start | bytes 589832 | tf_op jit(solution)/shard_map/weights/ppermute | solution.py:32
  25.4 10.6 %copy-start.1 = (bf16[256,2048]{1,0:T(8,128)(2,1)S(1)}, bf16[256,2048]{1,0:T(8,128)(2,1)}, u32[]{:S(2)}) copy-start(bf16[256,2048]{1,0:T(8,128)(2,1)} %param.10) | copy-start | bytes 3145732
  25.5 72.1 %copy-start.20 = (bf16[2048]{0:T(1024)(128)(2,1)S(1)}, bf16[2048]{0:T(1024)(128)(2,1)}, u32[]{:S(2)}) copy-start(bf16[2048]{0:T(1024)(128)(2,1)} %param.16) | copy-start | bytes 12292
  26.8 70.5 %all-to-all-start = ((f32[64,1,2048]{2,1,0:T(1,128)}), f32[64,1,2048]{2,1,0:T(1,128)S(1)}, u32[]{:S(2)}, u32[]{:S(2)}) async-start(f32[64,1,2048]{2,1,0:T(1,128)} %copy.46), calls=%async_computation | async-start | bytes 1048576 | tf_op jit(solution)/shard_map/direction/all_to_all | solution.py:90
  36.1 89.6 %collective-permute-start.4 = (bf16[256,2048]{1,0:T(8,128)(2,1)S(1)}, bf16[256,2048]{1,0:T(8,128)(2,1)S(1)}, u32[]{:S(2)}, u32[]{:S(2)}) collective-permute-start(bf16[256,2048]{1,0:T(8,128)(2,1)S(1)} %copy-done.1), channel_id=1, source_target_pairs={{0,2},{2,0},{1,3},{3,1},{4,6},{6,4},{5,7},{7,5},{8,10},{10,8},{9,1... | collective-permute-start | bytes 3145736 | tf_op jit(solution)/shard_map/tokens/ppermute | solution.py:79
  40.4 96.8 %collective-permute-start = (bf16[256,2048]{1,0:T(8,128)(2,1)S(1)}, bf16[256,2048]{1,0:T(8,128)(2,1)}, u32[]{:S(2)}, u32[]{:S(2)}) collective-permute-start(bf16[256,2048]{1,0:T(8,128)(2,1)S(1)} %copy-done.1), channel_id=1, source_target_pairs={{0,12},{1,5},{4,0},{5,9},{8,4},{9,13},{12,8},{13,1},{2,14},{3,7},{... | collective-permute-start | bytes 3145736 | tf_op jit(solution)/shard_map/tokens/ppermute | solution.py:32
  41.4 95.8 %collective-permute-start.2 = (bf16[256,2048]{1,0:T(8,128)(2,1)S(1)}, bf16[256,2048]{1,0:T(8,128)(2,1)}, u32[]{:S(2)}, u32[]{:S(2)}) collective-permute-start(bf16[256,2048]{1,0:T(8,128)(2,1)S(1)} %copy-done.1), channel_id=1, source_target_pairs={{0,5},{1,12},{4,9},{5,0},{8,13},{9,4},{12,1},{13,8},{2,7},{3,14},{... | collective-permute-start | bytes 3145736 | tf_op jit(solution)/shard_map/tokens/ppermute | solution.py:32
  98.3 32.6 %all-to-all-start.1 = ((f32[4,2,2048]{2,1,0:T(2,128)}), f32[4,2,2048]{2,1,0:T(2,128)S(1)}, u32[]{:S(2)}, u32[]{:S(2)}) async-start(f32[4,2,2048]{2,1,0:T(2,128)} %broadcast_in_dim.25), calls=%async_computation.1 | async-start | bytes 131072 | tf_op jit(solution)/shard_map/direction/all_to_all | solution.py:20
  125.6 41.2 %collective-permute-start.5 = (bf16[256,2048]{1,0:T(8,128)(2,1)S(1)}, bf16[256,2048]{1,0:T(8,128)(2,1)}, u32[]{:S(2)}, u32[]{:S(2)}) collective-permute-start(bf16[256,2048]{1,0:T(8,128)(2,1)S(1)} %collective-permute-done.4), channel_id=1, source_target_pairs={{0,12},{1,5},{4,0},{5,9},{8,4},{9,13},{12,8},{13,1},{2,14},{3,7},{... | collective-permute-start | bytes 3145736 | tf_op jit(solution)/shard_map/tokens/ppermute | solution.py:32
  126.7 40.1 %collective-permute-start.7 = (bf16[256,2048]{1,0:T(8,128)(2,1)S(1)}, bf16[256,2048]{1,0:T(8,128)(2,1)}, u32[]{:S(2)}, u32[]{:S(2)}) collective-permute-start(bf16[256,2048]{1,0:T(8,128)(2,1)S(1)} %collective-permute-done.4), channel_id=1, source_target_pairs={{0,5},{1,12},{4,9},{5,0},{8,13},{9,4},{12,1},{13,8},{2,7},{3,14},{... | collective-permute-start | bytes 3145736 | tf_op jit(solution)/shard_map/tokens/ppermute | solution.py:32
  131.7 24.0 %all-to-all-start.2 = ((f32[64,2,128]{2,1,0:T(2,128)}), f32[64,2,128]{2,1,0:T(2,128)}, u32[]{:S(2)}, u32[]{:S(2)}) async-start(f32[64,2,128]{2,1,0:T(2,128)} %copy.48), calls=%async_computation.2 | async-start | bytes 131072 | tf_op jit(solution)/shard_map/direction/all_to_all | solution.py:94
  140.3 39.9 %collective-permute-start.1 = (bf16[256,2048]{1,0:T(8,128)(2,1)}, bf16[256,2048]{1,0:T(8,128)(2,1)}, u32[]{:S(2)}, u32[]{:S(2)}) collective-permute-start(bf16[256,2048]{1,0:T(8,128)(2,1)} %get-tuple-element.48), channel_id=1, source_target_pairs={{0,13},{1,0},{4,1},{5,4},{8,5},{9,8},{12,9},{13,12},{2,15},{3,2},{... | collective-permute-start | bytes 3145736 | tf_op jit(solution)/shard_map/tokens/ppermute | solution.py:32
  140.3 39.9 %collective-permute-start.3 = (bf16[256,2048]{1,0:T(8,128)(2,1)}, bf16[256,2048]{1,0:T(8,128)(2,1)}, u32[]{:S(2)}, u32[]{:S(2)}) collective-permute-start(bf16[256,2048]{1,0:T(8,128)(2,1)} %collective-permute-done), channel_id=1, source_target_pairs={{1,5},{5,9},{9,13},{13,1},{3,7},{7,11},{11,15},{15,3},{17,21},{21,... | collective-permute-start | bytes 3145736 | tf_op jit(solution)/shard_map/tokens/ppermute | solution.py:32
  159.0 19.5 %all-to-all-start.3 = ((f32[64,1,1024]{2,1,0:T(1,128)}), f32[64,1,1024]{2,1,0:T(1,128)}, u32[]{:S(2)}, u32[]{:S(2)}) async-start(f32[64,1,1024]{2,1,0:T(1,128)} %copy.51), calls=%async_computation.3 | async-start | bytes 524288 | tf_op jit(solution)/shard_map/direction/all_to_all | solution.py:99
  166.8 7.1 %copy-start.19 = (bf16[8192]{0:T(1024)(128)(2,1)S(1)}, bf16[8192]{0:T(1024)(128)(2,1)}, u32[]{:S(2)}) copy-start(bf16[8192]{0:T(1024)(128)(2,1)} %param.11) | copy-start | bytes 49156
  170.2 15.2 %collective-permute-start.6 = (bf16[256,2048]{1,0:T(8,128)(2,1)}, bf16[256,2048]{1,0:T(8,128)(2,1)}, u32[]{:S(2)}, u32[]{:S(2)}) collective-permute-start(bf16[256,2048]{1,0:T(8,128)(2,1)} %get-tuple-element.45), channel_id=1, source_target_pairs={{0,13},{1,0},{4,1},{5,4},{8,5},{9,8},{12,9},{13,12},{2,15},{3,2},{... | collective-permute-start | bytes 3145736 | tf_op jit(solution)/shard_map/tokens/ppermute | solution.py:32
  170.6 17.3 %collective-permute-start.8 = (bf16[256,2048]{1,0:T(8,128)(2,1)}, bf16[256,2048]{1,0:T(8,128)(2,1)}, u32[]{:S(2)}, u32[]{:S(2)}) collective-permute-start(bf16[256,2048]{1,0:T(8,128)(2,1)} %collective-permute-done.5), channel_id=1, source_target_pairs={{1,5},{5,9},{9,13},{13,1},{3,7},{7,11},{11,15},{15,3},{17,21},{21,... | collective-permute-start | bytes 3145736 | tf_op jit(solution)/shard_map/tokens/ppermute | solution.py:32
  184.7 4.9 %copy-start.3 = (bf16[256,2048]{1,0:T(8,128)(2,1)S(1)}, bf16[256,2048]{1,0:T(8,128)(2,1)}, u32[]{:S(2)}) copy-start(bf16[256,2048]{1,0:T(8,128)(2,1)} %get-tuple-element.35) | copy-start | bytes 3145732
  184.7 4.9 %copy-start.4 = (bf16[256,2048]{1,0:T(8,128)(2,1)S(1)}, bf16[256,2048]{1,0:T(8,128)(2,1)}, u32[]{:S(2)}) copy-start(bf16[256,2048]{1,0:T(8,128)(2,1)} %get-tuple-element.36) | copy-start | bytes 3145732
  192.3 8.4 %copy-start.23 = (bf16[8192,768]{1,0:T(8,128)(2,1)S(1)}, bf16[8192,768]{1,0:T(8,128)(2,1)}, u32[]{:S(2)}) copy-start(bf16[8192,768]{1,0:T(8,128)(2,1)} %all-gather.2.cloned.1.call-done) | copy-start | bytes 37748740
  196.1 4.5 %copy-start.7 = (bf16[512,2048]{1,0:T(8,128)(2,1)S(1)}, bf16[512,2048]{1,0:T(8,128)(2,1)}, u32[]{:S(2)}) copy-start(bf16[512,2048]{1,0:T(8,128)(2,1)} %get-tuple-element.16) | copy-start | bytes 6291460
  218.5 9.9 %collective-permute-start.11 = (bf16[256,512]{1,0:T(8,128)(2,1)S(1)}, bf16[256,512]{1,0:T(8,128)(2,1)S(1)}, u32[]{:S(2)}, u32[]{:S(2)}) collective-permute-start(bf16[256,512]{1,0:T(8,128)(2,1)S(1)} %copy.59), channel_id=1, source_target_pairs={{0,0},{1,8},{4,4},{5,12},{8,9},{9,1},{12,13},{13,5},{2,2},{3,10},{... | collective-permute-start | bytes 786440 | tf_op jit(solution)/shard_map/return_heads/ppermute | solution.py:32
  220.8 9.1 %collective-permute-start.12 = (bf16[256,512]{1,0:T(8,128)(2,1)S(1)}, bf16[256,512]{1,0:T(8,128)(2,1)S(1)}, u32[]{:S(2)}, u32[]{:S(2)}) collective-permute-start(bf16[256,512]{1,0:T(8,128)(2,1)S(1)} %copy.60), channel_id=1, source_target_pairs={{0,4},{1,12},{4,8},{5,0},{8,13},{9,5},{12,1},{13,9},{2,6},{3,14},{... | collective-permute-start | bytes 786440 | tf_op jit(solution)/shard_map/return_heads/ppermute | solution.py:32
  230.0 39.9 %copy-start.10 = (f32[64,1,128]{2,1,0:T(1,128)S(1)}, f32[64,1,128]{2,1,0:T(1,128)}, u32[]{:S(2)}) copy-start(f32[64,1,128]{2,1,0:T(1,128)} %get-tuple-element.59) | copy-start | bytes 98308
  230.9 39.2 %copy-start.12 = (f32[64,1,128]{2,1,0:T(1,128)S(1)}, f32[64,1,128]{2,1,0:T(1,128)}, u32[]{:S(2)}) copy-start(f32[64,1,128]{2,1,0:T(1,128)} %copy-done.11) | copy-start | bytes 98308
  256.4 34.4 %copy-start.18 = (f32[1024]{0:T(1024)S(1)}, f32[1024]{0:T(1024)}, u32[]{:S(2)}) copy-start(f32[1024]{0:T(1024)} %reduce_sum.135) | copy-start | bytes 12292
  271.5 17.1 %all-to-all-start.6 = ((f32[64,1,1152]{2,1,0:T(1,128)}), f32[64,1,1152]{2,1,0:T(1,128)S(1)}, u32[]{:S(2)}, u32[]{:S(2)}) async-start(f32[64,1,1152]{2,1,0:T(1,128)} %copy.62), calls=%async_computation.6 | async-start | bytes 589824 | tf_op jit(solution)/shard_map/tail/all_to_all | solution.py:163
  (11 other events, 23.5 us)
Sparse Core Ops, SparseCore 0:
  22.5 139.8 all-gather.1
